TPU v7x, 128 devices: a whole 4x4x4 slice. The times are simulated.
128 devices in a mesh: rank: 8 (over x_hi, y), expert: 16 (over z, x_lo, core).
Axes of the slice: x: 4 (x_hi: 2, x_lo: 2; x = x_hi * 2 + x_lo), y: 4, z: 4, core: 2. Of those that a mesh axis runs over, the one named last changes fastest.
Arguments:
- hidden_in: bfloat16 [1024, 7168], P(('rank', 'expert')), may hold values from -6 to 6
- routes: int32 [1024, 8], P(('rank', 'expert')), may hold values from 0 to 15, all different within a row; in each aligned block of 8 rows (0 to 7, 8 to 15, ...) at most 5 rows name the same one
- gates: bfloat16 [1024, 8], P(('rank', 'expert')), may hold values from 0.049804688 to 0.59765625
- gate_proj: bfloat16 [16, 7168, 2048], P('expert', None, 'rank'), may hold values from -0.0625 to 0.0625
- up_proj: bfloat16 [16, 7168, 2048], P('expert', None, 'rank'), may hold values from -0.0625 to 0.0625
- down_proj: bfloat16 [16, 2048, 7168], P('expert', 'rank'), may hold values from -0.125 to 0.125
- query: bfloat16 [512, 128, 576], P(('rank', 'expert')), may hold values from -60 to 60
- kv_cache: bfloat16 [512, 1024, 576], P(('rank', 'expert')), may hold values from -6 to 6
- lengths: int32 [512], P(('rank', 'expert')), may hold values from 256 to 1024, as said below
- moving: int32 [128], P(('rank', 'expert')), may hold values from 0 to 3
- pair_mask: int32 [1], replicated, may hold values from 1 to 7
Outputs:
- routed: bfloat16 [1024, 7168], P(('rank', 'expert'))
- attention: bfloat16 [512, 128, 512], P(('rank', 'expert'))
- incoming: bfloat16 [128, 1024, 576], P(('rank', 'expert'))
Inputs may be any that keep to these rules, and one draw needn't show every extreme that they name: `routes`: in each aligned block of 8 rows (the tokens of one device) no expert is named by more than 5 rows. `lengths`: some request has length 1024. `moving`: indices among the 4 requests of the device. Rank r sends to and receives from rank r XOR pair_mask[0].
All inputs are finite; a program needn't handle non-finite values.
Results may differ from a plain program's by a relative error of at most 0.005.
Values may be sent and summed in bfloat16 or wider, within the bound.
A program may use at most 192 MiB of HBM per device.

v0:
```python
import jax
import jax.numpy as jnp
from jax import lax
from jax.sharding import PartitionSpec as P

LAT = 512
TOP = 8


score_scale = 192.0 ** (-0.5)


def from_partner(value, axis, apart):
    mask = 2**apart
    pairs = [(source, source ^ mask) for source in range(lax.axis_size(axis))]
    return lax.ppermute(value, axis, pairs)


def slot_table(dense_gate, capacity):
    is_member = (dense_gate > 0).astype(jnp.int32)
    earlier_count = jnp.cumsum(is_member, axis=0) - is_member
    slot_ids = jnp.arange(capacity, dtype=jnp.int32)
    member_t = jnp.transpose(is_member)[:, None, :] > 0
    earlier_t = jnp.transpose(earlier_count)[:, None, :]
    return member_t & (earlier_t == slot_ids[None, :, None])


def body(
    hidden_in,
    routes,
    gates,
    gate_proj,
    up_proj,
    down_proj,
    query,
    kv_cache,
    lengths,
    moving,
    pair_mask,
):
    tok_count = hidden_in.shape[0]
    feat_width = hidden_in.shape[1]
    rank_count = lax.axis_size("rank")
    experts = lax.axis_size("expert")
    capacity = min(tok_count, 5 * tok_count * TOP // (4 * experts))
    expert_ids = jnp.arange(experts, dtype=jnp.int32)
    named = routes[:, :, None] == expert_ids[None, None, :]
    dense_gate = jnp.sum(
        jnp.where(named, gates.astype(jnp.float32)[:, :, None], jnp.float32(0.0)), axis=1
    ).astype(jnp.bfloat16)
    w_gate = gate_proj[0]
    w_up = up_proj[0]
    w_down = down_proj[0]
    shared_rows, shared_gate = (
        lax.all_gather(hidden_in, "rank", axis=0, tiled=True),
        lax.all_gather(dense_gate, "rank", axis=0, tiled=True),
    )
    rank_rows = shared_rows.reshape(rank_count, tok_count, feat_width)
    rank_gate = shared_gate.reshape(rank_count, tok_count, experts)
    tables = jax.vmap(lambda gate_block: slot_table(gate_block, capacity))(rank_gate)
    buffer = jnp.einsum(
        "rect,rtd->recd", tables.astype(jnp.bfloat16), rank_rows, preferred_element_type=jnp.float32
    ).astype(jnp.bfloat16)
    slot_piece = lax.all_to_all(buffer, "expert", split_axis=1, concat_axis=1, tiled=True)
    piece_count = slot_piece.shape[0]
    slot_rows = slot_piece.reshape(-1, feat_width)
    gate_part = jnp.dot(slot_rows, w_gate, preferred_element_type=jnp.float32)
    up_part = jnp.dot(slot_rows, w_up, preferred_element_type=jnp.float32)
    hidden = (jax.nn.silu(gate_part) * up_part).astype(jnp.bfloat16)
    partial_out = jnp.dot(hidden, w_down, preferred_element_type=jnp.float32).reshape(
        piece_count, experts, capacity, feat_width
    )
    partials = lax.all_to_all(partial_out, "expert", split_axis=1, concat_axis=1, tiled=True)
    weighting = (
        tables.astype(jnp.float32)
        * jnp.transpose(rank_gate.astype(jnp.float32), (0, 2, 1))[:, :, None, :]
    )
    per_rank = jnp.einsum("rect,recd->rtd", weighting, partials, precision=lax.Precision.HIGHEST)
    routed = lax.psum_scatter(per_rank, "rank", scatter_dimension=0, tiled=True).reshape(
        tok_count, feat_width
    )
    routed_out = routed.astype(jnp.bfloat16)
    cache_slots = kv_cache.shape[1]
    positions = jnp.arange(cache_slots, dtype=jnp.int32)
    scores = (
        jnp.einsum("bhk,blk->bhl", query, kv_cache, preferred_element_type=jnp.float32)
        * score_scale
    )
    is_valid = positions[None, None, :] < lengths[:, None, None]
    scores = jnp.where(is_valid, scores, jnp.float32(-1e30))
    row_max = jnp.max(scores, axis=-1, keepdims=True)
    weights = jnp.where(is_valid, jnp.exp(scores - row_max), jnp.float32(0.0))
    denominator = jnp.sum(weights, axis=-1, keepdims=True)
    rounded = weights.astype(jnp.bfloat16)
    mixed = jnp.einsum(
        "bhl,blc->bhc", rounded, kv_cache[:, :, :LAT], preferred_element_type=jnp.float32
    )
    attention = (mixed / denominator).astype(jnp.bfloat16)
    picked = kv_cache[moving]
    picked_length = lengths[moving]
    in_length = positions[None, :] < picked_length[:, None]
    outgoing = jnp.where(in_length[:, :, None], picked, jnp.zeros_like(picked))
    travel = outgoing
    for bit_number in range(rank_count.bit_length() - 1):
        swapped = from_partner(travel, "rank", bit_number)
        bit_set = jnp.bitwise_and(jnp.right_shift(pair_mask[0], bit_number), 1)
        travel = jnp.where(bit_set == 1, swapped, travel)
    return (routed_out, attention, travel)


def solution(mesh):
    return jax.shard_map(
        body,
        mesh=mesh,
        in_specs=(
            P(("rank", "expert"), None),
            P(("rank", "expert"), None),
            P(("rank", "expert"), None),
            P("expert", None, "rank"),
            P("expert", None, "rank"),
            P("expert", "rank", None),
            P(("rank", "expert"), None, None),
            P(("rank", "expert"), None, None),
            P(("rank", "expert")),
            P(("rank", "expert")),
            P(),
        ),
        out_specs=(
            P(("rank", "expert"), None),
            P(("rank", "expert"), None, None),
            P(("rank", "expert"), None, None),
        ),
        check_vma=False,
    )
```

profile of v0, /device:TPU:1, one launch (start us, length us, event | category | flops | bytes accessed | tf_op | source)
XLA Modules:
  0.0 572.6 jit_solution(2473772694977026189)
XLA Ops:
  7.2 0.0 copy-start
  7.2 0.7 convert_element_type.36
  7.9 0.8 select_reduce_fusion
  8.7 26.5 %all_gather.6 = bf16[64,16]{1,0:T(8,128)(2,1)S(1)} all-gather(bf16[8,16]{1,0:T(8,128)(2,1)S(1)} %select_reduce_fusion), channel_id=1, replica_groups=mesh['rank'=8,'expert'=16] {'rank'}, dimensions={0}, use_global_device_ids=true | all-gather | bytes 2304 | tf_op jit(solution)/shard_map/all_gather | solution.py:56
  35.2 30.4 %all_gather.7 = bf16[64,7168]{1,0:T(8,128)(2,1)S(1)} all-gather(bf16[8,7168]{1,0:T(8,128)(2,1)} %param.11), channel_id=1, replica_groups=mesh['rank'=8,'expert'=16] {'rank'}, dimensions={0}, use_global_device_ids=true | all-gather | bytes 1032192 | tf_op jit(solution)/shard_map/all_gather | solution.py:55
  65.7 5.3 convolution_convert_fusion
  70.9 12.2 %copy.29 = bf16[8,16,5,7168]{3,0,2,1:T(8,128)(2,1)} copy(bf16[8,16,5,7168]{3,1,2,0:T(8,128)(2,1)} %convolution_convert_fusion) | data formatting | bytes 18350080 | tf_op jit(solution)/shard_map/convert_element_type | solution.py:63
  83.1 119.4 %all_to_all.10 = bf16[8,16,5,7168]{3,0,2,1:T(8,128)(2,1)S(1)} all-to-all(bf16[8,16,5,7168]{3,0,2,1:T(8,128)(2,1)} %copy.29), channel_id=1, replica_groups=mesh['rank'=8,'expert'=16] {'expert'}, dimensions={1} | all-to-all | bytes 18350080 | tf_op jit(solution)/shard_map/all_to_all | solution.py:64
  202.5 9.6 %copy.30 = bf16[8,16,5,7168]{3,2,1,0:T(8,128)(2,1)} copy(bf16[8,16,5,7168]{3,0,2,1:T(8,128)(2,1)S(1)} %all_to_all.10) | data formatting | bytes 18350080 | tf_op jit(solution)/shard_map/all_to_all | solution.py:64
  212.1 15.1 %reshape.109 = bf16[640,7168]{1,0:T(8,128)(2,1)} reshape(bf16[8,16,5,7168]{3,2,1,0:T(8,128)(2,1)} %copy.30) | data formatting | bytes 18350080 | tf_op jit(solution)/shard_map/reshape | solution.py:66
  227.2 0.0 copy-start.1
  227.2 0.0 copy-start.3
  227.2 7.3 %fusion.12 = f32[640,256]{1,0:T(8,128)S(1)} fusion(bf16[640,7168]{1,0:T(8,128)(2,1)} %reshape.109, bf16[1,7168,256]{2,1,0:T(8,128)(2,1)} %param.14), kind=kOutput, calls=%fused_computation.11 | convolution fusion | flops 2348810240 | bytes 13500416 | tf_op jit(solution)/shard_map/dot_general | solution.py:67
  234.5 0.0 copy-done.1
  234.5 1.0 copy-done.3
  235.5 2.5 fusion.18
  238.0 0.1 dot_general.26
  238.2 10.9 %fusion.8 = f32[8,16,5,7168]{3,0,2,1:T(8,128)} fusion(bf16[1,256,7168]{2,1,0:T(8,128)(2,1)} %param.16, bf16[8,16,5,256]{3,2,1,0:T(8,128)(2,1)S(1)} %dot_general.26), kind=kOutput, calls=%fused_computation.7 | convolution fusion | flops 2348810240 | bytes 22347776 | tf_op jit(solution)/shard_map/dot_general | solution.py:70
  249.1 0.0 copy-start.2
  249.1 6.1 %all-to-all-start.1 = ((f32[8,16,5,7168]{3,0,2,1:T(8,128)}), f32[8,16,5,7168]{3,0,2,1:T(8,128)}, u32[]{:S(2)}, u32[]{:S(2)}) async-start(f32[8,16,5,7168]{3,0,2,1:T(8,128)} %fusion.8), calls=%async_computation.1 | async-start | bytes 36700160 | tf_op jit(solution)/shard_map/all_to_all | solution.py:73
  255.2 0.0 reduce-scatter.2.cloned.1.call-start
  255.8 0.0 copy-done.2
  255.9 0.6 dynamic-slice.5
  256.4 0.6 iota_compare_fusion.3
  257.1 2.4 dynamic-slice_select_fusion
  259.5 0.0 collective-permute-start
  259.5 197.1 %all-to-all-done.1 = f32[8,16,5,7168]{3,0,2,1:T(8,128)} async-done(((f32[8,16,5,7168]{3,0,2,1:T(8,128)}), f32[8,16,5,7168]{3,0,2,1:T(8,128)}, u32[]{:S(2)}, u32[]{:S(2)}) %all-to-all-start.1) | async-done | bytes 18350112 | tf_op jit(solution)/shard_map/all_to_all | solution.py:73
  456.6 28.1 %fusion.3 = f32[8,8,7168]{2,1,0:T(8,128)} fusion(f32[8,16,5,7168]{3,0,2,1:T(8,128)} %all-to-all-done.1, f32[8,16,8]{1,2,0:T(8,128)S(1)} %convert_bitcast_fusion.1, s32[8,16,8]{1,2,0:T(8,128)S(1)} %subtract_bitcast_fusion, pred[8,16,8]{1,2,0:T(8,128)(4,1)S(1)} %compare_bitcast_fusion), kind=kOutput, calls=%fused_computation.4 | convolution fusion | flops 440417280 | bytes 20194304 | tf_op jit(solution)/shard_map/rect,recd->rtd/dot_general | solution.py:78
  484.7 0.0 reduce-scatter.2.cloned.1.call-update
  485.4 0.0 collective-permute-done
  485.4 1.4 broadcast_select_fusion
  486.8 0.4 collective-permute-start.1
  487.2 35.2 %collective-permute-done.1 = bf16[1,1024,576]{1,2,0:T(8,128)(2,1)S(1)} collective-permute-done((bf16[1,1024,576]{1,2,0:T(8,128)(2,1)S(1)}, bf16[1,1024,576]{1,2,0:T(8,128)(2,1)S(1)}, u32[]{:S(2)}, u32[]{:S(2)}) %collective-permute-start.1) | collective-permute-done | bytes 1179680 | tf_op jit(solution)/shard_map/ppermute | solution.py:16
  522.4 0.1 broadcast_select_fusion.1
  522.5 2.5 collective-permute-start.2
  525.0 0.1 iota_compare_fusion.2
  525.1 0.0 copy-done
  525.1 4.9 fusion.44
  530.0 4.9 divide_convert_fusion
  534.9 18.2 %collective-permute-done.2 = bf16[1,1024,576]{1,2,0:T(8,128)(2,1)S(1)} collective-permute-done((bf16[1,1024,576]{1,2,0:T(8,128)(2,1)S(1)}, bf16[1,1024,576]{1,2,0:T(8,128)(2,1)S(1)}, u32[]{:S(2)}, u32[]{:S(2)}) %collective-permute-start.2) | collective-permute-done | bytes 1179680 | tf_op jit(solution)/shard_map/ppermute | solution.py:16
  553.1 1.1 broadcast_select_fusion.2
  554.3 9.9 %reduce-scatter.2.cloned.1.call-done = f32[1,8,7168]{2,1,0:T(8,128)} async-done(((f32[8,8,7168]{2,1,0:T(8,128)}), f32[1,8,7168]{2,1,0:T(8,128)}) %reduce-scatter.2.cloned.1.call-update) | async-done | bytes 229392 | tf_op jit(solution)/shard_map/reduce_scatter | solution.py:79
  564.1 1.6 convert_bitcast_fusion
  (5 shorter events, 0.1 us)
Async XLA Ops:
  7.2 518.0 %copy-start = (bf16[4,128,576]{1,2,0:T(8,128)(2,1)S(1)}, bf16[4,128,576]{1,2,0:T(8,128)(2,1)}, u32[]{:S(2)}) copy-start(bf16[4,128,576]{1,2,0:T(8,128)(2,1)} %param.17) | copy-start | bytes 1769476
  227.2 7.3 %copy-start.1 = (bf16[640,7168]{1,0:T(8,128)(2,1)S(1)}, bf16[640,7168]{1,0:T(8,128)(2,1)}, u32[]{:S(2)}) copy-start(bf16[640,7168]{1,0:T(8,128)(2,1)} %reshape.109) | copy-start | bytes 27525124
  227.2 8.3 %copy-start.3 = (bf16[1,7168,256]{2,1,0:T(8,128)(2,1)S(1)}, bf16[1,7168,256]{2,1,0:T(8,128)(2,1)}, u32[]{:S(2)}) copy-start(bf16[1,7168,256]{2,1,0:T(8,128)(2,1)} %param.15) | copy-start | bytes 11010052
  249.1 6.8 %copy-start.2 = (s32[4]{0:T(128)S(1)}, s32[4]{0:T(128)}, u32[]{:S(2)}) copy-start(s32[4]{0:T(128)} %param.19) | copy-start | bytes 52
  249.1 207.5 %all-to-all-start.1 = ((f32[8,16,5,7168]{3,0,2,1:T(8,128)}), f32[8,16,5,7168]{3,0,2,1:T(8,128)}, u32[]{:S(2)}, u32[]{:S(2)}) async-start(f32[8,16,5,7168]{3,0,2,1:T(8,128)} %fusion.8), calls=%async_computation.1 | async-start | bytes 36700160 | tf_op jit(solution)/shard_map/all_to_all | solution.py:73
  255.2 309.0 %reduce-scatter.2.cloned.1.call-start = ((), (), s32[]{:S(2)}) async-start(), calls=%async_computation.3 | async-start | bytes 2064384 | tf_op jit(solution)/shard_map/reduce_scatter | solution.py:79
  259.5 225.9 %collective-permute-start = (bf16[1,1024,576]{1,2,0:T(8,128)(2,1)}, bf16[1,1024,576]{1,2,0:T(8,128)(2,1)S(1)}, u32[]{:S(2)}, u32[]{:S(2)}) collective-permute-start(bf16[1,1024,576]{1,2,0:T(8,128)(2,1)} %dynamic-slice_select_fusion), channel_id=1, source_target_pairs={{0,16},{16,0},{32,48},{48,32},{64,80},{80,64},{96,112},{112,96},{1... | collective-permute-start | bytes 3538952 | tf_op jit(solution)/shard_map/ppermute | solution.py:16
  486.8 35.6 %collective-permute-start.1 = (bf16[1,1024,576]{1,2,0:T(8,128)(2,1)S(1)}, bf16[1,1024,576]{1,2,0:T(8,128)(2,1)S(1)}, u32[]{:S(2)}, u32[]{:S(2)}) collective-permute-start(bf16[1,1024,576]{1,2,0:T(8,128)(2,1)S(1)} %broadcast_select_fusion), channel_id=1, source_target_pairs={{0,32},{16,48},{32,0},{48,16},{64,96},{80,112},{96,64},{112,80},{1... | collective-permute-start | bytes 3538952 | tf_op jit(solution)/shard_map/ppermute | solution.py:16
  522.5 30.6 %collective-permute-start.2 = (bf16[1,1024,576]{1,2,0:T(8,128)(2,1)S(1)}, bf16[1,1024,576]{1,2,0:T(8,128)(2,1)S(1)}, u32[]{:S(2)}, u32[]{:S(2)}) collective-permute-start(bf16[1,1024,576]{1,2,0:T(8,128)(2,1)S(1)} %broadcast_select_fusion.1), channel_id=1, source_target_pairs={{0,64},{16,80},{32,96},{48,112},{64,0},{80,16},{96,32},{112,48},{1... | collective-permute-start | bytes 3538952 | tf_op jit(solution)/shard_map/ppermute | solution.py:16
Sparse Core Ops, SparseCore 0:
  484.9 79.2 reduce-scatter.1
where the time goes:
time: 574 us; the launch traced here: 573 us
  waiting for transfers between devices  260 us (45%)
  blocking collectives  176 us (31%)
  matrix products  63.9 us (11%)
  local copies, waits for them, and re-layouts  38.5 us (7%)
  between operations  15.4 us (3%)
  starting transfers between devices  9.04 us (2%)
  other arithmetic  8.95 us (2%)
    all_to_all x1, waiting for transfers between devices, body(): lax.all_to_all(partial_out, 'expert', split_axis=1, concat_axis=1, tiled=...  197 us
    all_to_all x1, blocking collectives, body(): lax.all_to_all(buffer, 'expert', split_axis=1, concat_axis=1, tiled=True)  119 us
    ppermute x3, waiting for transfers between devices, from_partner(): return lax.ppermute(value, axis, pairs)  53.4 us
    all_gather x1, blocking collectives, body(): lax.all_gather(hidden_in, 'rank', axis=0, tiled=True)  30.4 us
    dot_general x1, matrix products, body(): jnp.einsum('rect,recd->rtd', weighting, partials, precision=lax.Precision...  28.1 us
    all_gather x1, blocking collectives, body(): lax.all_gather(dense_gate, 'rank', axis=0, tiled=True)  26.5 us
    reshape x1, local copies, waits for them, and re-layouts, body(): slot_rows = slot_piece.reshape(-1, feat_width)  15.1 us
    convert_element_type x1, local copies, waits for them, and re-layouts, body(): buffer = jnp.einsum('rect,rtd->recd', tables.astype(jnp.bfloat16), rank_r...  12.2 us
  transfers between devices with their start and end apart: 5, of which 4 were waited for; matrix products, arithmetic and copies ran while one was open for 8% of the time, Pallas kernels for 0%

commit v1 on v0

v1 whole, which is shorter than its diff:
```python
import functools

import jax
import jax.numpy as jnp
from jax import lax
from jax.experimental import pallas as pl
from jax.experimental.pallas import tpu as pltpu
from jax.sharding import PartitionSpec as P

LAT = 512
SCALE = 192.0 ** (-0.5)
MESH = pl.DeviceIdType.MESH
F32 = jnp.float32
BF16 = jnp.bfloat16
GATE_TILE = 128

DIMS = ((1, 0, 2), (2, 1, 0), (0, 2, 1))
GATE_PART = 2


def part_sizes(half):
    if half == 3584:
        return (1536, 1024, 1024)
    return (half // 3,) * 3


def kernel(
    hid_ref, routes_ref, gates_ref, wg_ref, wu_ref, wd_ref, q_ref, kv_ref, len_ref, mov_ref, mask_ref,
    routed_ref, att_ref, inc_ref,
    x0, x1, x2, w, dn, acc, rb, h, gbuf, tmp,
    f3_0, f3_1, f3_2, r3p_0, r3p_1, r3p_2, r3m_0, r3m_1, r3m_2, t2_0, t2_1, t2_2,
    s2_0, s2_1, s2_2, q2_0, q2_1, q2_2, t1_0, t1_1, t1_2, s1_0, s1_1, s1_2, q1_0, q1_1, q1_2,
    stage_s, stage_r, fin, finr, kvv, qv,
    ya1, ya2, za1, za2, va1, va2, ua, sa, yb1, yb2, zb1, zb2, vb1, vb2, ub, sb,
    send_sems, recv_sems, local_sems,
):
    half = hid_ref.shape[1] // 2
    sizes = part_sizes(half)
    starts = (0, sizes[0], sizes[0] + sizes[1])
    xs, f3, r3p, r3m = (x0, x1, x2), (f3_0, f3_1, f3_2), (r3p_0, r3p_1, r3p_2), (r3m_0, r3m_1, r3m_2)
    t2, s2, q2 = (t2_0, t2_1, t2_2), (s2_0, s2_1, s2_2), (q2_0, q2_1, q2_2)
    t1, s1, q1 = (t1_0, t1_1, t1_2), (s1_0, s1_1, s1_2), (q1_0, q1_1, q1_2)
    ff = wg_ref.shape[1]

    r = lax.axis_index("rank")
    e = lax.axis_index("expert")
    c = e % 2
    oc = 1 - c
    y = r % 4
    z = e // 4
    x = (r // 4) * 2 + (e // 2) % 2
    pos = (x, y, z)

    def at_chip(px, py, pz, core):
        return ((px // 2) * 4 + py, pz * 4 + (px % 2) * 2 + core)

    def nb(dim, delta):
        moved = [(v + delta + 4) % 4 if i == dim else v for i, v in enumerate(pos)]
        return at_chip(*moved, c)

    sibling = at_chip(x, y, z, oc)
    y_one = at_chip(x, y + 1 - 2 * (y % 2), z, c)
    y_three = at_chip(x, 3 - y, z, c)

    counter = [0]
    started = []

    def rc(src, dst, device):
        i = counter[0]
        counter[0] += 1
        return pltpu.make_async_remote_copy(
            src_ref=src, dst_ref=dst, send_sem=send_sems.at[i], recv_sem=recv_sems.at[i],
            device_id=device, device_id_type=MESH,
        )

    def go(src, dst, device):
        d = rc(src, dst, device)
        d.start()
        started.append(d)
        return d

    def done_sending():
        for d in started:
            d.wait_send()
        started.clear()

    locals_ = []

    def lc(src, dst):
        d = pltpu.make_async_copy(src, dst, local_sems.at[len(locals_)])
        locals_.append(d)
        d.start()
        return d

    lkv = lc(kv_ref, kvv)
    lq = lc(q_ref, qv)
    mine = pl.ds(pl.multiple_of(c * half, 128), half)
    other = pl.ds(pl.multiple_of(oc * half, 128), half)
    lwg = lc(wg_ref.at[mine, :], w.at[2 * c])
    lwu = lc(wu_ref.at[mine, :], w.at[2 * c + 1])
    lwd = lc(wd_ref.at[:, mine], dn.at[c])

    lane = lax.broadcasted_iota(jnp.int32, (8, GATE_TILE), 1)
    gate_rows = jnp.zeros((8, GATE_TILE), F32)
    wide_gates = gates_ref[...].astype(F32)
    names = routes_ref[...]
    for k in range(routes_ref.shape[1]):
        gate_rows = gate_rows + jnp.where(lane == names[:, k : k + 1], wide_gates[:, k : k + 1], 0.0)
    stage_s[:, pl.ds(0, half)] = hid_ref[:, other]
    stage_s[:, pl.ds(half, GATE_TILE)] = gate_rows.astype(BF16)

    barrier = pltpu.get_barrier_semaphore()
    for device in (nb(0, 1), nb(0, -1), nb(1, 1), nb(1, -1), nb(2, 1), nb(2, -1), sibling):
        pl.semaphore_signal(barrier, inc=1, device_id=device, device_id_type=MESH)
    pl.semaphore_wait(barrier, 7)

    tok = go(stage_s, stage_r, sibling)
    rwg = go(wg_ref.at[other, :], w.at[2 * c], sibling)
    rwu = go(wu_ref.at[other, :], w.at[2 * c + 1], sibling)
    rwd = go(wd_ref.at[:, other], dn.at[c], sibling)

    tok.wait_recv()
    cf = c.astype(F32)
    own_wide = jnp.concatenate([hid_ref[:, mine].astype(F32), gate_rows], axis=1)
    got_wide = stage_r[...].astype(F32)
    top = own_wide * (1.0 - cf) + got_wide * cf
    bottom = got_wide * (1.0 - cf) + own_wide * cf
    block = jnp.concatenate([top, bottom], axis=0).astype(BF16)

    def place(p):
        return tuple(pos[d] for d in DIMS[p])

    def near(v, delta):
        return (v + delta + 4) % 4

    for p in range(3):
        a1, a2, a3 = place(p)
        end = half + GATE_TILE if p == GATE_PART else starts[p] + sizes[p]
        xs[p][a3, a2, a1] = block[:, starts[p] : end]

    g1 = []
    for p in range(3):
        a1, a2, a3 = place(p)
        own = xs[p].at[a3, a2, a1]
        g1.append((go(own, own, nb(DIMS[p][0], 1)), go(own, own, nb(DIMS[p][0], -1))))

    mask = mask_ref[0]
    m_y = mask % 4
    m_x = mask // 4
    sub = ya1.shape[1]
    step_rows = 64 if sub % 64 == 0 else 16

    def for_rows(fn):
        @pl.loop(0, sub // step_rows)
        def _(i):
            fn(pl.ds(pl.multiple_of(i * step_rows, 16), step_rows))

    def pick_rows(dst, dst_slot, part):
        which = mov_ref[0]
        limit = len_ref[which]

        def one(rows):
            first = part * sub + rows.start
            piece = kvv[which, pl.ds(pl.multiple_of(first, 16), step_rows), :].astype(F32)
            at = lax.broadcasted_iota(jnp.int32, piece.shape, 0) + first
            dst[dst_slot, rows, :] = jnp.where(at < limit, piece, 0.0).astype(BF16)

        for_rows(one)

    def move_rows(dst, src, src_slot):
        def one(rows):
            dst[rows, :] = src[src_slot, rows, :]

        for_rows(one)

    def y_first(b1, b2):
        return go(b1.at[0], b1.at[1], y_one), go(b2.at[0], b2.at[1], y_three)

    def y_second(b1, b2, z1, z2, stage, first):
        first[0].wait_recv()
        first[1].wait_recv()
        move_rows(stage.at[0], b1, jnp.where(m_y == 3, 0, 1))
        s3 = go(stage.at[0], z1.at[1], y_three)
        move_rows(stage.at[1], b2, jnp.where(m_y == 1, 0, 1))
        s1_ = go(stage.at[1], z2.at[1], y_one)
        move_rows(z1.at[0], b1, jnp.where(m_y == 1, 1, 0))
        move_rows(z2.at[0], b2, jnp.where(m_y == 3, 1, 0))
        return s3, s1_

    def y_end(z1, z2, second, dst1, dst2):
        second[0].wait_recv()
        second[1].wait_recv()
        move_rows(dst1, z1, jnp.where(m_y <= 1, 0, 1))
        move_rows(dst2, z2, jnp.where((m_y == 0) | (m_y == 3), 0, 1))

    def x_first(v1, v2, u):
        return go(v1.at[0], u.at[0], nb(0, 1)), go(v2.at[0], u.at[1], nb(0, -1))

    def x_second(v1, v2, u, first):
        first[0].wait_recv()
        a = go(u.at[0], v1.at[1], nb(0, 1))
        first[1].wait_recv()
        return a, go(u.at[1], v2.at[1], nb(0, -1))

    def x_end(v1, v2, second, dst1, dst2):
        second[0].wait_recv()
        second[1].wait_recv()
        move_rows(dst1, v1, m_x)
        move_rows(dst2, v2, m_x)

    lkv.wait()
    pick_rows(ya1, 0, 0)
    pick_rows(ya2, 0, 1)
    mig_a = y_first(ya1, ya2)
    pick_rows(vb1, 0, 2)
    pick_rows(vb2, 0, 3)
    mig_b = x_first(vb1, vb2, ub)

    g1f = []
    for p in range(3):
        a1, a2, a3 = place(p)
        cut = xs[p].shape[4] // 256 * 128
        rest = xs[p].shape[4] - cut
        g1[p][0].wait_recv()
        left = xs[p].at[a3, a2, near(a1, -1), :, pl.ds(0, cut)]
        one = go(left, left, nb(DIMS[p][0], 1))
        g1[p][1].wait_recv()
        right = xs[p].at[a3, a2, near(a1, 1), :, pl.ds(cut, rest)]
        g1f.append((one, go(right, right, nb(DIMS[p][0], -1))))

    lq.wait()

    def attend(b):
        kv = kvv[b]
        scores = lax.dot_general(qv[b], kv, (((1,), (1,)), ((), ())), preferred_element_type=F32) * SCALE
        valid = lax.broadcasted_iota(jnp.int32, scores.shape, 1) < len_ref[b]
        scores = jnp.where(valid, scores, -1e30)
        top_score = jnp.max(scores, axis=-1, keepdims=True)
        weights = jnp.where(valid, jnp.exp(scores - top_score), 0.0)
        total = jnp.sum(weights, axis=-1, keepdims=True)
        mixed = jnp.dot(weights.astype(BF16), kv[:, :LAT], preferred_element_type=F32)
        att_ref[b] = (mixed / total).astype(BF16)

    g2, g3 = [], [[None] * 4 for _ in range(3)]
    offs = (0, -1, 1, 2)

    def third(p, k):
        a1, a2, a3 = place(p)
        line = xs[p].at[a3, near(a2, offs[k])]
        g3[p][k] = (go(line, line, nb(DIMS[p][2], 1)), go(line, line, nb(DIMS[p][2], -1)))

    for p in range(3):
        a1, a2, a3 = place(p)
        g1f[p][0].wait_recv()
        g1f[p][1].wait_recv()
        line = xs[p].at[a3, a2]
        g2.append((go(line, line, nb(DIMS[p][1], 1)), go(line, line, nb(DIMS[p][1], -1))))
    for p in range(3):
        third(p, 0)

    @pl.loop(0, 4)
    def _(n):
        for i in range(4):
            for j in range(4):
                acc[n, i, j] = jnp.zeros(acc.shape[3:], F32)

    attend(0)

    g2f = []
    for p in range(3):
        a1, a2, a3 = place(p)
        g2[p][0].wait_recv()
        left = xs[p].at[a3, near(a2, -1), pl.ds(0, 2)]
        one = go(left, left, nb(DIMS[p][1], 1))
        g2[p][1].wait_recv()
        right = xs[p].at[a3, near(a2, 1), pl.ds(2, 2)]
        g2f.append((one, go(right, right, nb(DIMS[p][1], -1))))
        third(p, 1)
        third(p, 2)

    attend(1)
    g3f = [[None] * 4 for _ in range(3)]

    def forward(p, k):
        a1, a2, a3 = place(p)
        g3[p][k][0].wait_recv()
        g3[p][k][1].wait_recv()
        delta = 1 if k % 2 == 0 else -1
        line = xs[p].at[near(a3, -delta), near(a2, offs[k])]
        g3f[p][k] = go(line, line, nb(DIMS[p][2], delta))

    for p in range(3):
        g2f[p][0].wait_recv()
        g2f[p][1].wait_recv()
        third(p, 3)
        forward(p, 0)

    mig_a = y_second(ya1, ya2, za1, za2, sa, mig_a)
    mig_b = x_second(vb1, vb2, ub, mig_b)

    def rows_of(p, j):
        full = slice(None)
        if p == 0:
            return [(i, full, j) for i in range(4)]
        if p == 1:
            return [(j, i, full) for i in range(4)]
        return [(full, j, i) for i in range(4)]

    lwg.wait()
    lwu.wait()
    rwg.wait_recv()
    rwu.wait_recv()

    def project(p, j):
        lhs = xs[p][j][:, :, :, : sizes[p]].reshape(256, sizes[p])

        @pl.loop(0, 4)
        def _(n):
            res = jnp.dot(lhs, w[n, pl.ds(starts[p], sizes[p]), :], preferred_element_type=F32)
            res = res.reshape(4, 4, 16, ff)
            for i, index in enumerate(rows_of(p, j)):
                acc[(n, *index)] = acc[(n, *index)] + res[i]

    for p in range(3):
        project(p, place(p)[2])
    for p in range(3):
        forward(p, 1)
    attend(2)
    for p in range(3):
        forward(p, 2)
    attend(3)
    for p in range(3):
        forward(p, 3)
    for p in range(3):
        project(p, near(place(p)[2], 1))
        project(p, near(place(p)[2], -1))
    y_end(za1, za2, mig_a, va1.at[0], va2.at[0])
    mig_a = x_first(va1, va2, ua)
    x_end(vb1, vb2, mig_b, yb1.at[0], yb2.at[0])
    mig_b = y_first(yb1, yb2)
    for p in range(3):
        for k in range(4):
            g3f[p][k].wait_recv()
        project(p, near(place(p)[2], 2))

    for n in range(2):
        pick = lax.broadcasted_iota(jnp.int32, (GATE_TILE, GATE_TILE), 0) == e - c + n
        pick = jnp.where(pick, 1.0, 0.0).astype(BF16)
        for j in range(4):
            table = xs[GATE_PART][j][:, :, :, sizes[GATE_PART] :].reshape(256, GATE_TILE)
            spread = jnp.dot(table, pick, preferred_element_type=F32).reshape(4, 4, 16, GATE_TILE)
            for i, index in enumerate(rows_of(GATE_PART, j)):
                gbuf[(n, *index)] = spread[i]

    part_sends = []
    for k in (3, 1, 2, 0):
        xx = near(x, offs[k])
        part_sends.append(
            go(acc.at[pl.ds(2 * oc, 2), xx], rb.at[:, xx], sibling)
        )
    hid_sends = []
    for at, k in enumerate((3, 1, 2, 0)):
        xx = near(x, offs[k])
        part_sends[at].wait_recv()
        gate = acc[2 * c, xx] + rb[0, xx]
        up = acc[2 * c + 1, xx] + rb[1, xx]
        h[c, xx] = (gate * (1.0 / (1.0 + jnp.exp(-gate))) * up).astype(BF16)
        hid_sends.append(go(h.at[c, xx], h.at[c, xx], sibling))

    lwd.wait()
    rwd.wait_recv()
    done_sending()
    for d in hid_sends:
        d.wait_recv()

    def down(p, j, dst):
        def pull(ref, n):
            return jnp.concatenate([ref[(n, *i)].reshape(64, ref.shape[-1]) for i in rows_of(p, j)], axis=0)

        hs = [pull(h, n) for n in range(2)]
        gs = [pull(gbuf, n) for n in range(2)]
        gs = [jnp.concatenate([g, g], axis=1) for g in gs]

        @pl.loop(0, sizes[p] // 256)
        def _(n):
            cols = pl.ds(pl.multiple_of(starts[p] + n * 256, 128), 256)
            out = gs[0] * jnp.dot(hs[0], dn[0, :, cols], preferred_element_type=F32)
            out = out + gs[1] * jnp.dot(hs[1], dn[1, :, cols], preferred_element_type=F32)
            dst[:, :, pl.ds(pl.multiple_of(n * 256, 128), 256)] = out.reshape(4, 64, 256)

    roffs = (2, -1, 1, 0)
    fw3 = [[None] * 4 for _ in range(3)]

    def slot(p, which, k):
        return xs[p].at[which, k, :, :, pl.ds(0, sizes[p])]

    def put(p, which, k, value):
        xs[p][which, k, :, :, : sizes[p]] = value.astype(BF16).reshape(4, 16, sizes[p])

    for p in range(3):
        a1, a2, a3 = place(p)
        view = tmp.at[:, :, pl.ds(0, sizes[p])]
        down(p, near(a3, 2), view)
        for k in range(4):
            put(p, 0, k, view[near(a2, roffs[k])])
            fw3[p][k] = go(slot(p, 0, k), f3[p].at[k], nb(DIMS[p][2], 1 if k % 2 == 0 else -1))

    sp, sm = [[None] * 4 for _ in range(3)], [[None] * 4 for _ in range(3)]
    for p in range(3):
        a1, a2, a3 = place(p)
        view = tmp.at[:, :, pl.ds(0, sizes[p])]
        for side, which, sent, back in ((1, 1, sp, r3p), (-1, 2, sm, r3m)):
            down(p, near(a3, side), view)
            summed = (0, 2) if side == 1 else (1, 3)
            alone = (1, 3) if side == 1 else (0, 2)
            for k in alone + summed:
                value = view[near(a2, roffs[k])]
                if k in summed:
                    fw3[p][k].wait_recv()
                    value = value + f3[p][k].reshape(64, sizes[p]).astype(F32)
                put(p, which, k, value)
                sent[p][k] = go(slot(p, which, k), back[p].at[k], nb(DIMS[p][2], side))
    for p in range(3):
        down(p, place(p)[2], t2[p])

    mig_a = x_second(va1, va2, ua, mig_a)
    mig_b = y_second(yb1, yb2, zb1, zb2, sb, mig_b)

    def settle(p, k):
        a1, a2, a3 = place(p)
        sp[p][k].wait_recv()
        sm[p][k].wait_recv()
        got = r3p[p][k].reshape(64, sizes[p]).astype(F32) + r3m[p][k].reshape(64, sizes[p]).astype(F32)
        return t2[p][near(a2, roffs[k])] + got

    fw2 = []
    for p in range(3):
        d = DIMS[p][1]
        s2[p][0] = settle(p, 0).astype(BF16)
        top_half, low_half = pl.ds(0, 32), pl.ds(32, 32)
        fw2.append((
            go(s2[p].at[0, top_half], q2[p].at[0, top_half], nb(d, 1)),
            go(s2[p].at[0, low_half], q2[p].at[0, low_half], nb(d, -1)),
        ))
    back2 = [[None, None] for _ in range(3)]
    for p in range(3):
        d = DIMS[p][1]
        value = settle(p, 1)
        fw2[p][1].wait_recv()
        s2[p][2, pl.ds(0, 32), :] = value[:32].astype(BF16)
        s2[p][2, pl.ds(32, 32), :] = (value[32:] + q2[p][0, pl.ds(32, 32), :].astype(F32)).astype(BF16)
        back2[p][1] = go(s2[p].at[2], q2[p].at[2], nb(d, -1))
    for p in range(3):
        d = DIMS[p][1]
        value = settle(p, 2)
        fw2[p][0].wait_recv()
        s2[p][1, pl.ds(0, 32), :] = (value[:32] + q2[p][0, pl.ds(0, 32), :].astype(F32)).astype(BF16)
        s2[p][1, pl.ds(32, 32), :] = value[32:].astype(BF16)
        back2[p][0] = go(s2[p].at[1], q2[p].at[1], nb(d, 1))

    fw1, back1 = [], []
    for p in range(3):
        a1, a2, a3 = place(p)
        d = DIMS[p][0]
        value = settle(p, 3)
        back2[p][0].wait_recv()
        back2[p][1].wait_recv()
        value = value + q2[p][1].astype(F32) + q2[p][2].astype(F32)
        t1[p][...] = value.reshape(4, 16, sizes[p])
        s1[p][0] = t1[p][near(a1, 2)].astype(BF16)
        cut = sizes[p] // 2
        left, right = pl.ds(0, cut), pl.ds(cut, cut)
        fw1.append((
            go(s1[p].at[0, :, left], q1[p].at[0, :, left], nb(d, 1)),
            go(s1[p].at[0, :, right], q1[p].at[0, :, right], nb(d, -1)),
        ))
    for p in range(3):
        a1, a2, a3 = place(p)
        d = DIMS[p][0]
        cut = sizes[p] // 2
        fw1[p][0].wait_recv()
        value = t1[p][near(a1, 1)]
        s1[p][1, :, pl.ds(0, cut)] = (value[:, :cut] + q1[p][0, :, pl.ds(0, cut)].astype(F32)).astype(BF16)
        s1[p][1, :, pl.ds(cut, cut)] = value[:, cut:].astype(BF16)
        one = go(s1[p].at[1], q1[p].at[1], nb(d, 1))
        fw1[p][1].wait_recv()
        value = t1[p][near(a1, -1)]
        s1[p][2, :, pl.ds(0, cut)] = value[:, :cut].astype(BF16)
        s1[p][2, :, pl.ds(cut, cut)] = (value[:, cut:] + q1[p][0, :, pl.ds(cut, cut)].astype(F32)).astype(BF16)
        back1.append((one, go(s1[p].at[2], q1[p].at[2], nb(d, -1))))

    def out_rows(part):
        return inc_ref.at[pl.ds(part * sub, sub), :]

    x_end(va1, va2, mig_a, out_rows(0), out_rows(1))
    y_end(zb1, zb2, mig_b, out_rows(2), out_rows(3))

    for p in range(3):
        a1, a2, a3 = place(p)
        back1[p][0].wait_recv()
        back1[p][1].wait_recv()
        fin[:, pl.ds(starts[p], sizes[p])] = (
            t1[p][a1] + q1[p][1].astype(F32) + q1[p][2].astype(F32)
        )
    last = go(fin.at[pl.ds(pl.multiple_of(8 * oc, 8), 8), :], finr, sibling)
    routed_ref[:, mine] = fin[pl.ds(pl.multiple_of(8 * c, 8), 8), :].astype(BF16)
    last.wait_recv()
    routed_ref[:, other] = finr[...].astype(BF16)
    done_sending()


def body(hidden_in, routes, gates, gate_proj, up_proj, down_proj, query, kv_cache, lengths, moving, pair_mask):
    tokens, width = hidden_in.shape
    half = width // 2
    sizes = part_sizes(half)
    ff = gate_proj.shape[2]
    requests, slots, kvw = kv_cache.shape
    heads = query.shape[1]
    sub = slots // 4

    def per_part(*lead, dtype=BF16, extra=False):
        return [
            pltpu.VMEM((*lead, s + (GATE_TILE if extra and p == GATE_PART else 0)), dtype)
            for p, s in enumerate(sizes)
        ]

    mig = (
        [pltpu.VMEM((2, sub, kvw), BF16)] * 8
    )
    scratch = [
        *per_part(4, 4, 4, 16, extra=True),
        pltpu.VMEM((4, half, ff), BF16),
        pltpu.VMEM((2, ff, half), BF16),
        pltpu.VMEM((4, 4, 4, 4, 16, ff), F32),
        pltpu.VMEM((2, 4, 4, 4, 16, ff), F32),
        pltpu.VMEM((2, 4, 4, 4, 16, ff), BF16),
        pltpu.VMEM((2, 4, 4, 4, 16, GATE_TILE), F32),
        pltpu.VMEM((4, 64, max(sizes)), F32),
        *per_part(4, 4, 16),
        *per_part(4, 4, 16),
        *per_part(4, 4, 16),
        *per_part(4, 64, dtype=F32),
        *per_part(3, 64),
        *per_part(3, 64),
        *per_part(4, 16, dtype=F32),
        *per_part(3, 16),
        *per_part(3, 16),
        pltpu.VMEM((8, half + GATE_TILE), BF16),
        pltpu.VMEM((8, half + GATE_TILE), BF16),
        pltpu.VMEM((16, half), F32),
        pltpu.VMEM((8, half), F32),
        pltpu.VMEM((requests, slots, kvw), BF16),
        pltpu.VMEM((requests, heads, kvw), BF16),
        *mig,
        *mig,
        pltpu.SemaphoreType.DMA((160,)),
        pltpu.SemaphoreType.DMA((160,)),
        pltpu.SemaphoreType.DMA((8,)),
    ]
    vmem = pl.BlockSpec(memory_space=pltpu.VMEM)
    smem = pl.BlockSpec(memory_space=pltpu.SMEM)
    anywhere = pl.BlockSpec(memory_space=pl.ANY)
    routed, attention, incoming = pl.pallas_call(
        kernel,
        out_shape=(
            jax.ShapeDtypeStruct((tokens, width), BF16),
            jax.ShapeDtypeStruct((requests, heads, LAT), BF16),
            jax.ShapeDtypeStruct((slots, kvw), BF16),
        ),
        in_specs=[vmem, vmem, vmem, anywhere, anywhere, anywhere, anywhere, anywhere, smem, smem, smem],
        out_specs=(vmem, vmem, vmem),
        scratch_shapes=scratch,
        compiler_params=pltpu.CompilerParams(
            collective_id=0, has_side_effects=True, vmem_limit_bytes=64 * 1024 * 1024
        ),
        cost_estimate=pl.CostEstimate(flops=13_000_000_000, bytes_accessed=20_000_000, transcendentals=800_000),
    )(
        hidden_in, routes, gates, gate_proj[0], up_proj[0], down_proj[0], query, kv_cache, lengths, moving, pair_mask
    )
    return routed, attention, incoming[None]


def solution(mesh):
    return jax.shard_map(
        body,
        mesh=mesh,
        in_specs=(
            P(("rank", "expert"), None),
            P(("rank", "expert"), None),
            P(("rank", "expert"), None),
            P("expert", None, "rank"),
            P("expert", None, "rank"),
            P("expert", "rank", None),
            P(("rank", "expert"), None, None),
            P(("rank", "expert"), None, None),
            P(("rank", "expert")),
            P(("rank", "expert")),
            P(),
        ),
        out_specs=(
            P(("rank", "expert"), None),
            P(("rank", "expert"), None, None),
            P(("rank", "expert"), None, None),
        ),
        check_vma=False,
    )
```

time: 574 us -> 143 us (0.25)
  waiting for transfers between devices: 260 us -> 0 us
  blocking collectives: 176 us -> 0 us
  Pallas kernels: 0 us -> 125 us
  matrix products: 63.9 us -> 0 us
  local copies, waits for them, and re-layouts: 38.5 us -> 15.6 us
  between operations: 15.4 us -> 1.93 us
  starting transfers between devices: 9.04 us -> 0 us
  other arithmetic: 8.95 us -> 0 us
    all_to_all x1 -> x0, waiting for transfers between devices: 197 us -> none  [body(): lax.all_to_all(partial_out, 'expert', split_axis=1, concat_axis=1, tiled=...]
    pallas_call x0 -> x1, Pallas kernels: none -> 125 us  [body(): pl.pallas_call(kernel, out_shape=(jax.ShapeDtypeStruct((tokens, width), B...]
    all_to_all x1 -> x0, blocking collectives: 119 us -> none  [body(): lax.all_to_all(buffer, 'expert', split_axis=1, concat_axis=1, tiled=True)]
    dot_general x6 -> x0, matrix products: 59 us -> none  [the longest x1 28.1 us: body(): jnp.einsum('rect,recd->rtd', weighting, partials, precision=lax.Precision...]
    all_gather x2 -> x0, blocking collectives: 56.9 us -> none  [the longest x1 30.4 us: body(): lax.all_gather(hidden_in, 'rank', axis=0, tiled=True)]
    ppermute x3 -> x0, waiting for transfers between devices: 53.4 us -> none  [from_partner(): return lax.ppermute(value, axis, pairs)]
    reshape x1 -> x0, local copies, waits for them, and re-layouts: 15.1 us -> none  [body(): slot_rows = slot_piece.reshape(-1, feat_width)]
    unnamed x8 -> x5, local copies, waits for them, and re-layouts: 0.98 us -> 15.6 us
  transfers between devices with their start and end apart: 5 -> 0, of which waited for: 4 -> 0; matrix products, arithmetic and copies ran while one was open for 8% -> 0% of each run, Pallas kernels for 0% -> 0%
where the time goes in v1:
time: 143 us
  Pallas kernels  125 us (87%)
  local copies, waits for them, and re-layouts  15.6 us (11%)
  between operations  1.93 us (1%)
    pallas_call x1, Pallas kernels, body(): pl.pallas_call(kernel, out_shape=(jax.ShapeDtypeStruct((tokens, width), B...  125 us
    unnamed x5, local copies, waits for them, and re-layouts  15.6 us

profile of v1, /device:TPU:1, one launch (start us, length us, event | category | flops | bytes accessed | tf_op | source)
XLA Modules:
  0.0 142.8 jit_solution(5952496805098890360)
XLA Ops:
  1.9 2.1 %copy.14.q_ref = bf16[4,128,576]{2,1,0:T(8,128)(2,1)} copy(bf16[4,128,576]{1,2,0:T(8,128)(2,1)} %param.17) | data formatting | bytes 1179648 | tf_op args[6]
  4.1 7.7 %copy.15.kv_ref = bf16[4,1024,576]{2,1,0:T(8,128)(2,1)} copy(bf16[4,1024,576]{1,2,0:T(8,128)(2,1)} %param.18) | data formatting | bytes 9437184 | tf_op args[7]
  11.8 125.2 %shard_map.130 = (bf16[8,7168]{1,0:T(8,128)(2,1)}, bf16[4,128,512]{2,1,0:T(8,128)(2,1)}, bf16[1024,576]{1,0:T(8,128)(2,1)}) custom-call(bf16[8,7168]{1,0:T(8,128)(2,1)} %hid_ref.1, s32[8,8]{1,0:T(8,128)} %routes_ref.1, bf16[8,8]{1,0:T(8,128)(2,1)} %gates_ref.1, bf16[7168,256]{1,0:T(8,128)(2,1)} %bitcast.5, bf16[7168,256]{1,0:T(8,128)(2,1)} %bitcast.6, ...), custom_call_target="tpu_custom_call" | custom-call | flops 12999999488 | bytes 20000000 | tf_op jit(solution)/shard_map/pallas_call | solution.py:563
  137.0 2.4 %copy.16 = bf16[1,1024,576]{1,2,0:T(8,128)(2,1)} copy(bf16[1,1024,576]{2,1,0:T(8,128)(2,1)} %bitcast.4) | data formatting | bytes 2359296
  139.4 1.6 %copy.21 = bf16[8,7168]{1,0:T(8,128)(2,1)} copy(bf16[8,7168]{1,0:T(8,128)(2,1)} %get-tuple-element.15) | data formatting | bytes 229376
  140.9 1.9 %copy.22 = bf16[4,128,512]{2,1,0:T(8,128)(2,1)} copy(bf16[4,128,512]{2,1,0:T(8,128)(2,1)} %get-tuple-element.16) | data formatting | bytes 1048576

commit v2 on v1

v2 whole, which is shorter than its diff:
```python
import functools

import jax
import jax.numpy as jnp
from jax import lax
from jax.experimental import pallas as pl
from jax.experimental.pallas import tpu as pltpu
from jax.sharding import PartitionSpec as P

LAT = 512
SCALE = 192.0 ** (-0.5)
MESH = pl.DeviceIdType.MESH
F32 = jnp.float32
BF16 = jnp.bfloat16
GATE_TILE = 128

DIMS = ((1, 0, 2), (2, 1, 0), (0, 2, 1))
GATE_PART = 2


def part_sizes(half):
    if half == 3584:
        return (1792, 896, 896)
    return (half // 3,) * 3


def kernel(
    hid_ref, routes_ref, gates_ref, wg_ref, wu_ref, wd_ref, q_ref, kv_ref, len_ref, mov_ref, mask_ref,
    routed_ref, att_ref, inc_ref,
    x0, x1, x2, w, dn, acc, rb, h, gbuf, tmp,
    f3_0, f3_1, f3_2, r3p_0, r3p_1, r3p_2, r3m_0, r3m_1, r3m_2, t2_0, t2_1, t2_2,
    s2_0, s2_1, s2_2, q2_0, q2_1, q2_2, s1_0, s1_1, s1_2, q1_0, q1_1, q1_2,
    stage_s, stage_r, fin, finr, kvv, qv,
    ya1, ya2, za1, za2, va1, va2, ua, sa, yb1, yb2, zb1, zb2, vb1, vb2, ub, sb,
    send_sems, recv_sems, local_sems,
):
    half = hid_ref.shape[1] // 2
    sizes = part_sizes(half)
    starts = (0, sizes[0], sizes[0] + sizes[1])
    xs, f3, r3p, r3m = (x0, x1, x2), (f3_0, f3_1, f3_2), (r3p_0, r3p_1, r3p_2), (r3m_0, r3m_1, r3m_2)
    t2, s2, q2 = (t2_0, t2_1, t2_2), (s2_0, s2_1, s2_2), (q2_0, q2_1, q2_2)
    s1, q1 = (s1_0, s1_1, s1_2), (q1_0, q1_1, q1_2)
    ff = wg_ref.shape[1]

    r = lax.axis_index("rank")
    e = lax.axis_index("expert")
    c = e % 2
    oc = 1 - c
    y = r % 4
    z = e // 4
    x = (r // 4) * 2 + (e // 2) % 2
    pos = (x, y, z)

    def at_chip(px, py, pz, core):
        return ((px // 2) * 4 + py, pz * 4 + (px % 2) * 2 + core)

    def nb(dim, delta):
        moved = [(v + delta + 4) % 4 if i == dim else v for i, v in enumerate(pos)]
        return at_chip(*moved, c)

    sibling = at_chip(x, y, z, oc)
    y_one = at_chip(x, y + 1 - 2 * (y % 2), z, c)
    y_three = at_chip(x, 3 - y, z, c)

    counter = [0]
    started = []

    def rc(src, dst, device):
        i = counter[0]
        counter[0] += 1
        return pltpu.make_async_remote_copy(
            src_ref=src, dst_ref=dst, send_sem=send_sems.at[i], recv_sem=recv_sems.at[i],
            device_id=device, device_id_type=MESH,
        )

    def go(src, dst, device):
        d = rc(src, dst, device)
        d.start()
        started.append(d)
        return d

    def done_sending():
        for d in started:
            d.wait_send()
        started.clear()

    locals_ = []

    def lc(src, dst):
        d = pltpu.make_async_copy(src, dst, local_sems.at[len(locals_)])
        locals_.append(d)
        d.start()
        return d

    lkv = lc(kv_ref, kvv)
    lq = lc(q_ref, qv)
    mine = pl.ds(pl.multiple_of(c * half, 128), half)
    other = pl.ds(pl.multiple_of(oc * half, 128), half)

    lane = lax.broadcasted_iota(jnp.int32, (8, GATE_TILE), 1)
    gate_rows = jnp.zeros((8, GATE_TILE), F32)
    wide_gates = gates_ref[...].astype(F32)
    names = routes_ref[...]
    for k in range(routes_ref.shape[1]):
        gate_rows = gate_rows + jnp.where(lane == names[:, k : k + 1], wide_gates[:, k : k + 1], 0.0)
    stage_s[:, pl.ds(0, half)] = hid_ref[:, other]
    stage_s[:, pl.ds(half, GATE_TILE)] = gate_rows.astype(BF16)

    barrier = pltpu.get_barrier_semaphore()
    for device in (nb(0, 1), nb(0, -1), nb(1, 1), nb(1, -1), nb(2, 1), nb(2, -1), sibling):
        pl.semaphore_signal(barrier, inc=1, device_id=device, device_id_type=MESH)
    pl.semaphore_wait(barrier, 7)

    tok = go(stage_s, stage_r, sibling)
    tok.wait_recv()
    cf = c.astype(F32)
    own_wide = jnp.concatenate([hid_ref[:, mine].astype(F32), gate_rows], axis=1)
    got_wide = stage_r[...].astype(F32)
    top = own_wide * (1.0 - cf) + got_wide * cf
    bottom = got_wide * (1.0 - cf) + own_wide * cf
    block = jnp.concatenate([top, bottom], axis=0).astype(BF16)

    def place(p):
        return tuple(pos[d] for d in DIMS[p])

    def near(v, delta):
        return (v + delta + 4) % 4

    for p in range(3):
        a1, a2, a3 = place(p)
        end = half + GATE_TILE if p == GATE_PART else starts[p] + sizes[p]
        xs[p][a3, a2, a1] = block[:, starts[p] : end]

    offs = (0, -1, 1, 2)

    def both_ways(ref, dim):
        return go(ref, ref, nb(dim, 1)), go(ref, ref, nb(dim, -1))

    g1, g2, g3 = [], [[None] * 4 for _ in range(3)], [[None] * 4 for _ in range(3)]
    own3 = [[None] * 4 for _ in range(3)]

    def block_at(p, k):
        a1, a2, a3 = place(p)
        return xs[p].at[a3, a2, near(a1, offs[k])]

    def second(p, k):
        g2[p][k] = both_ways(block_at(p, k), DIMS[p][1])

    def third_own(p, k):
        own3[p][k] = both_ways(block_at(p, k), DIMS[p][2])

    def third_line(p, k):
        a1, a2, a3 = place(p)
        g3[p][k] = both_ways(xs[p].at[a3, near(a2, offs[k])], DIMS[p][2])

    def side_of(k):
        return 1 if k % 2 == 0 else -1

    for p in range(3):
        g1.append(both_ways(block_at(p, 0), DIMS[p][0]))
    for p in range(3):
        second(p, 0)
    for p in range(3):
        third_own(p, 0)

    gate_cols = pl.ds(pl.multiple_of(2 * c * ff, 128), ff)
    up_cols = pl.ds(pl.multiple_of((2 * c + 1) * ff, 128), ff)
    lwg = lc(wg_ref.at[mine, :], w.at[:, gate_cols])
    lwu = lc(wu_ref.at[mine, :], w.at[:, up_cols])
    lwd = lc(wd_ref.at[:, mine], dn.at[c])
    rwg = go(wg_ref.at[other, :], w.at[:, gate_cols], sibling)
    rwu = go(wu_ref.at[other, :], w.at[:, up_cols], sibling)
    rwd = go(wd_ref.at[:, other], dn.at[c], sibling)

    mask = mask_ref[0]
    m_y = mask % 4
    m_x = mask // 4
    sub = ya1.shape[1]
    step_rows = 48 if sub % 48 == 0 else 16

    def for_rows(fn):
        @pl.loop(0, sub // step_rows)
        def _(i):
            fn(pl.ds(pl.multiple_of(i * step_rows, 16), step_rows))

    def pick_rows(dst, dst_slot, part):
        which = mov_ref[0]
        limit = len_ref[which]

        def one(rows):
            first = part * sub + rows.start
            piece = kvv[which, pl.ds(pl.multiple_of(first, 16), step_rows), :].astype(F32)
            at = lax.broadcasted_iota(jnp.int32, piece.shape, 1)
            dst[dst_slot, rows, :] = jnp.where(at < limit, piece, 0.0).astype(BF16)

        for_rows(one)

    def move_rows(dst, src, src_slot):
        def one(rows):
            dst[rows, :] = src[src_slot, rows, :]

        for_rows(one)

    def y_first(b1, b2):
        return go(b1.at[0], b1.at[1], y_one), go(b2.at[0], b2.at[1], y_three)

    def y_second(b1, b2, z1, z2, stage, first):
        first[0].wait_recv()
        first[1].wait_recv()
        move_rows(stage.at[0], b1, jnp.where(m_y == 3, 0, 1))
        s3 = go(stage.at[0], z1.at[1], y_three)
        move_rows(stage.at[1], b2, jnp.where(m_y == 1, 0, 1))
        s1_ = go(stage.at[1], z2.at[1], y_one)
        move_rows(z1.at[0], b1, jnp.where(m_y == 1, 1, 0))
        move_rows(z2.at[0], b2, jnp.where(m_y == 3, 1, 0))
        return s3, s1_

    def y_end(z1, z2, second, dst1, dst2):
        second[0].wait_recv()
        second[1].wait_recv()
        move_rows(dst1, z1, jnp.where(m_y <= 1, 0, 1))
        move_rows(dst2, z2, jnp.where((m_y == 0) | (m_y == 3), 0, 1))

    def x_first(v1, v2, u):
        return go(v1.at[0], u.at[0], nb(0, 1)), go(v2.at[0], u.at[1], nb(0, -1))

    def x_second(v1, v2, u, first):
        first[0].wait_recv()
        a = go(u.at[0], v1.at[1], nb(0, 1))
        first[1].wait_recv()
        return a, go(u.at[1], v2.at[1], nb(0, -1))

    def x_end(v1, v2, second, dst1, dst2):
        second[0].wait_recv()
        second[1].wait_recv()
        move_rows(dst1, v1, m_x)
        move_rows(dst2, v2, m_x)

    g1f = []
    for p in range(3):
        a1, a2, a3 = place(p)
        cut = xs[p].shape[4] // 256 * 128
        rest = xs[p].shape[4] - cut
        g1[p][0].wait_recv()
        left = xs[p].at[a3, a2, near(a1, -1), :, pl.ds(0, cut)]
        one = go(left, left, nb(DIMS[p][0], 1))
        g1[p][1].wait_recv()
        right = xs[p].at[a3, a2, near(a1, 1), :, pl.ds(cut, rest)]
        g1f.append((one, go(right, right, nb(DIMS[p][0], -1))))
    for p in range(3):
        second(p, 1)
        second(p, 2)
    for p in range(3):
        third_own(p, 1)
        third_own(p, 2)

    lq.wait()
    lkv.wait()

    def attend(b):
        kv = kvv[b]
        scores = lax.dot_general(qv[b], kv, (((0,), (0,)), ((), ())), preferred_element_type=F32) * SCALE
        valid = lax.broadcasted_iota(jnp.int32, scores.shape, 1) < len_ref[b]
        scores = jnp.where(valid, scores, -1e30)
        top_score = jnp.max(scores, axis=-1, keepdims=True)
        weights = jnp.where(valid, jnp.exp(scores - top_score), 0.0)
        total = jnp.sum(weights, axis=-1, keepdims=True)
        mixed = lax.dot_general(
            weights.astype(BF16), kv[:LAT, :], (((1,), (1,)), ((), ())), preferred_element_type=F32
        )
        att_ref[b] = (mixed / total).astype(BF16)

    g2f, own3f, g3f = ([[None] * 4 for _ in range(3)] for _ in range(3))

    def arrived(pair, k):
        pair[0 if k % 2 == 0 else 1].wait_recv()

    def rest_arrived(pair, k):
        pair[1 if k % 2 == 0 else 0].wait_recv()

    def second_on(p, k):
        a1, a2, a3 = place(p)
        arrived(g2[p][k], k)
        ref = xs[p].at[a3, near(a2, -side_of(k)), near(a1, offs[k])]
        g2f[p][k] = go(ref, ref, nb(DIMS[p][1], side_of(k)))

    def own_on(p, k):
        a1, a2, a3 = place(p)
        arrived(own3[p][k], k)
        ref = xs[p].at[near(a3, -side_of(k)), a2, near(a1, offs[k])]
        own3f[p][k] = go(ref, ref, nb(DIMS[p][2], side_of(k)))

    def line_on(p, k):
        a1, a2, a3 = place(p)
        arrived(g3[p][k], k)
        ref = xs[p].at[near(a3, -side_of(k)), near(a2, offs[k])]
        g3f[p][k] = (go(ref, ref, nb(DIMS[p][2], side_of(k))),)

    for p in range(3):
        second_on(p, 0)
    for p in range(3):
        own_on(p, 0)
    for p in range(3):
        g1f[p][0].wait_recv()
        g1f[p][1].wait_recv()
        second(p, 3)
    for p in range(3):
        third_own(p, 3)

    attend(0)

    for p in range(3):
        second_on(p, 1)
        second_on(p, 2)
    for p in range(3):
        own_on(p, 1)
        own_on(p, 2)

    @pl.loop(0, 4)
    def _(i):
        for j in range(4):
            acc[i, j] = jnp.zeros(acc.shape[2:], F32)

    for p in range(3):
        second_on(p, 3)
        for k in range(4):
            rest_arrived(g2[p][k], k)
        third_line(p, 1)
        third_line(p, 2)
    for p in range(3):
        own_on(p, 3)

    attend(1)

    for p in range(3):
        for k in range(4):
            g2f[p][k].wait_recv()
        third_line(p, 3)

    pick_rows(ya1, 0, 0)
    pick_rows(ya2, 0, 1)
    mig_a = y_first(ya1, ya2)
    pick_rows(vb1, 0, 2)
    pick_rows(vb2, 0, 3)
    mig_b = x_first(vb1, vb2, ub)

    def rows_of(p, j):
        full = slice(None)
        if p == 0:
            return [(i, full, j) for i in range(4)]
        if p == 1:
            return [(j, i, full) for i in range(4)]
        return [(full, j, i) for i in range(4)]

    lwg.wait()
    lwu.wait()
    rwg.wait_recv()
    rwu.wait_recv()

    def index_of(p, i3, i2):
        full = slice(None)
        return ((i2, full, i3), (i3, i2, full), (full, i3, i2))[p]

    def project(p, lines):
        lhs = jnp.concatenate(
            [xs[p][i3, i2, :, :, : sizes[p]].reshape(64, sizes[p]) for i3, i2 in lines], axis=0
        )

        res = jnp.dot(lhs, w[pl.ds(starts[p], sizes[p]), :], preferred_element_type=F32)
        for i, line in enumerate(lines):
            at = index_of(p, *line)
            acc[at] = acc[at] + res[64 * i : 64 * i + 64].reshape(4, 16, 4 * ff)

    def lines_at(p, delta, which):
        a1, a2, a3 = place(p)
        return [(near(a3, delta), near(a2, offs[k])) for k in which]

    for p in range(3):
        line_on(p, 1)
        line_on(p, 2)
    for p in range(3):
        project(p, lines_at(p, 0, range(4)))
    attend(2)
    for p in range(3):
        a1, a2, a3 = place(p)
        g3[p][3][0].wait_recv()
        left = xs[p].at[near(a3, -1), near(a2, 2), pl.ds(0, 2)]
        one = go(left, left, nb(DIMS[p][2], 1))
        g3[p][3][1].wait_recv()
        right = xs[p].at[near(a3, 1), near(a2, 2), pl.ds(2, 2)]
        g3f[p][3] = (one, go(right, right, nb(DIMS[p][2], -1)))
    mig_a = y_second(ya1, ya2, za1, za2, sa, mig_a)
    mig_b = x_second(vb1, vb2, ub, mig_b)
    for p in range(3):
        for k in range(4):
            rest_arrived(own3[p][k], k)
        rest_arrived(g3[p][1], 1)
        rest_arrived(g3[p][2], 2)
        project(p, lines_at(p, -1, range(4)) + lines_at(p, 1, range(4)))
    attend(3)
    for p in (1, 2, 0):
        for k in range(4):
            own3f[p][k].wait_recv()
        for k in (1, 2):
            g3f[p][k][0].wait_recv()
        project(p, lines_at(p, 2, range(3)))
    lwd.wait()
    rwd.wait_recv()
    for p in (1, 2, 0):
        for d in g3f[p][3]:
            d.wait_recv()
        project(p, lines_at(p, 2, (3,)))

    part_sends = []
    for k in (3, 1, 2, 0):
        xx = near(x, offs[k])
        part_sends.append(
            go(acc.at[xx, :, :, :, pl.ds(pl.multiple_of(2 * oc * ff, 128), 2 * ff)], rb.at[xx], sibling)
        )

    for n in range(2):
        pick = lax.broadcasted_iota(jnp.int32, (GATE_TILE, GATE_TILE), 0) == e - c + n
        pick = jnp.where(pick, 1.0, 0.0).astype(BF16)
        for j in range(4):
            table = xs[GATE_PART][j][:, :, :, sizes[GATE_PART] :].reshape(256, GATE_TILE)
            spread = jnp.dot(table, pick, preferred_element_type=F32).reshape(4, 4, 16, GATE_TILE)
            for i, index in enumerate(rows_of(GATE_PART, j)):
                gbuf[(n, *index)] = spread[i]

    hid_sends = []
    for at, k in enumerate((3, 1, 2, 0)):
        xx = near(x, offs[k])
        part_sends[at].wait_recv()
        gate = acc[xx, :, :, :, gate_cols] + rb[xx, :, :, :, :ff]
        up = acc[xx, :, :, :, up_cols] + rb[xx, :, :, :, ff:]
        h[c, xx] = (gate * (1.0 / (1.0 + jnp.exp(-gate))) * up).astype(BF16)
        hid_sends.append(go(h.at[c, xx], h.at[c, xx], sibling))
    done_sending()

    def down(p, j, dst):
        def pull(ref, n):
            return jnp.concatenate([ref[(n, *i)].reshape(64, ref.shape[-1]) for i in rows_of(p, j)], axis=0)

        hs = [pull(h, n) for n in range(2)]
        gs = [pull(gbuf, n) for n in range(2)]
        most = 896 if sizes[p] % 896 == 0 else 256
        gs = [jnp.concatenate([g] * (most // GATE_TILE), axis=1) for g in gs]

        def tile(first, width):
            cols = pl.ds(pl.multiple_of(starts[p] + first, 128), width)
            out = gs[0][:, :width] * jnp.dot(hs[0], dn[0, :, cols], preferred_element_type=F32)
            out = out + gs[1][:, :width] * jnp.dot(hs[1], dn[1, :, cols], preferred_element_type=F32)
            at = pl.ds(pl.multiple_of(first, 128), width)
            if dst.dtype == BF16:
                dst[:, :, :, at] = out.astype(BF16).reshape(4, 4, 16, width)
            else:
                dst[:, :, at] = out.reshape(4, 64, width)

        for first in range(0, sizes[p], most):
            tile(first, most)

    def cut_of(p):
        return sizes[p] // 256 * 128

    roffs = (2, -1, 1, 0)

    def down_to_tmp(p, j):
        view = tmp.at[:, :, pl.ds(0, sizes[p])]
        down(p, j, view)
        return view

    def put(p, which, k2, value):
        xs[p][which, k2, :, :, : sizes[p]] = value.astype(BF16).reshape(4, 16, sizes[p])

    def put_block(p, which, k2, i1, value):
        xs[p][which, k2, i1, :, : sizes[p]] = value.astype(BF16)

    def send3(p, which, k2, blocks, into, side):
        src = xs[p].at[which, k2, blocks, :, pl.ds(0, sizes[p])]
        return go(src, into[p].at[k2, blocks], nb(DIMS[p][2], side))

    fw3 = [[None] * 8 for _ in range(3)]
    hid_sends[0].wait_recv()
    for p in (1, 0, 2):
        a1, a2, a3 = place(p)
        if p == 0:
            for d in hid_sends[1:]:
                d.wait_recv()
        down(p, near(a3, 2), xs[p].at[0])

        def forward3(i2, blocks, into, side):
            src = xs[p].at[0, i2, blocks, :, pl.ds(0, sizes[p])]
            return go(src, f3[p].at[into, blocks], nb(DIMS[p][2], side))

        far = near(a2, 2)
        fw3[p][0] = (forward3(far, pl.ds(0, 2), 0, 1), forward3(far, pl.ds(2, 2), 0, -1))
        for k in (1, 2):
            fw3[p][k] = forward3(near(a2, roffs[k]), pl.ds(0, 4), k, side_of(k))
        for k in range(4):
            fw3[p][4 + k] = forward3(a2, near(a1, roffs[k]), 3, side_of(k))

    y_end(za1, za2, mig_a, va1.at[0], va2.at[0])
    mig_a = x_first(va1, va2, ua)
    x_end(vb1, vb2, mig_b, yb1.at[0], yb2.at[0])
    mig_b = y_first(yb1, yb2)

    to_side = {1: [[None] * 8 for _ in range(3)], -1: [[None] * 8 for _ in range(3)]}
    back3 = {1: r3p, -1: r3m}
    for p in (1, 2, 0):
        a1, a2, a3 = place(p)
        for side, which in ((1, 1), (-1, 2)):
            sent = to_side[side][p]
            view = down_to_tmp(p, near(a3, side))
            fw3[p][0][0 if side == 1 else 1].wait_recv()
            value = view[near(a2, 2)]
            first = 0 if side == 1 else 2
            added = f3[p][0, pl.ds(first, 2)].reshape(32, sizes[p]).astype(F32)
            if side == 1:
                value = jnp.concatenate([value[:32] + added, value[32:]], axis=0)
            else:
                value = jnp.concatenate([value[:32], value[32:] + added], axis=0)
            put(p, which, 0, value)
            sent[0] = send3(p, which, 0, pl.ds(0, 4), back3[side], side)
            for k in (1, 2):
                value = view[near(a2, roffs[k])]
                if side_of(k) == side:
                    fw3[p][k].wait_recv()
                    value = value + f3[p][k].reshape(64, sizes[p]).astype(F32)
                put(p, which, k, value)
                sent[k] = send3(p, which, k, pl.ds(0, 4), back3[side], side)
            for k in range(4):
                i1 = near(a1, roffs[k])
                value = view[a2, pl.ds(pl.multiple_of(i1 * 16, 16), 16), :]
                if side_of(k) == side:
                    fw3[p][4 + k].wait_recv()
                    value = value + f3[p][3, i1].astype(F32)
                put_block(p, which, 3, i1, value)
                sent[4 + k] = send3(p, which, 3, i1, back3[side], side)
    for p in (1, 2, 0):
        down(p, place(p)[2], t2[p])

    mig_a = x_second(va1, va2, ua, mig_a)
    mig_b = y_second(yb1, yb2, zb1, zb2, sb, mig_b)

    def settle(p, k):
        i2 = near(place(p)[1], roffs[k])
        to_side[1][p][k].wait_recv()
        to_side[-1][p][k].wait_recv()
        got = r3p[p][k].reshape(64, sizes[p]).astype(F32) + r3m[p][k].reshape(64, sizes[p]).astype(F32)
        t2[p][i2] = t2[p][i2] + got

    def t2_block(p, k, i1):
        return t2[p][near(place(p)[1], roffs[k]), pl.ds(pl.multiple_of(i1 * 16, 16), 16), :]

    def send2(p, which, i1, side):
        return go(s2[p].at[which, i1], q2[p].at[which, i1], nb(DIMS[p][1], side))

    fw2 = [[None] * 4 for _ in range(3)]
    for p in (1, 2, 0):
        settle(p, 0)
        for k in range(4):
            i1 = near(place(p)[0], roffs[k])
            s2[p][0, i1] = t2_block(p, 0, i1).astype(BF16)
            fw2[p][k] = send2(p, 0, i1, side_of(k))
    back2 = [[[None] * 4, [None] * 4] for _ in range(3)]
    for p in (1, 2, 0):
        settle(p, 1)
        settle(p, 2)
        for k in range(4):
            i1 = near(place(p)[0], roffs[k])
            fw2[p][k].wait_recv()
            for slot, side, line in ((1, 1, 2), (2, -1, 1)):
                value = t2_block(p, line, i1)
                if side_of(k) == side:
                    value = value + q2[p][0, i1].astype(F32)
                s2[p][slot, i1] = value.astype(BF16)
                back2[p][slot - 1][k] = send2(p, slot, i1, side)

    def settle_block(p, k):
        i1 = near(place(p)[0], roffs[k])
        to_side[1][p][4 + k].wait_recv()
        to_side[-1][p][4 + k].wait_recv()
        value = t2_block(p, 3, i1) + r3p[p][3, i1].astype(F32) + r3m[p][3, i1].astype(F32)
        back2[p][0][k].wait_recv()
        back2[p][1][k].wait_recv()
        return value + q2[p][1, i1].astype(F32) + q2[p][2, i1].astype(F32)

    fw1, back1 = [None] * 3, [[None, None] for _ in range(3)]
    for p in (1, 2, 0):
        d = DIMS[p][0]
        s1[p][0] = settle_block(p, 0).astype(BF16)
        cut = cut_of(p)
        left, right = pl.ds(0, cut), pl.ds(cut, sizes[p] - cut)
        fw1[p] = (
            go(s1[p].at[0, :, left], q1[p].at[0, :, left], nb(d, 1)),
            go(s1[p].at[0, :, right], q1[p].at[0, :, right], nb(d, -1)),
        )
    for p in (1, 2, 0):
        d = DIMS[p][0]
        cut = cut_of(p)
        value = settle_block(p, 1)
        fw1[p][1].wait_recv()
        s1[p][2, :, pl.ds(0, cut)] = value[:, :cut].astype(BF16)
        s1[p][2, :, pl.ds(cut, sizes[p] - cut)] = (value[:, cut:] + q1[p][0, :, pl.ds(cut, sizes[p] - cut)].astype(F32)).astype(BF16)
        back1[p][1] = go(s1[p].at[2], q1[p].at[2], nb(d, -1))
    for p in (1, 2, 0):
        d = DIMS[p][0]
        cut = cut_of(p)
        value = settle_block(p, 2)
        fw1[p][0].wait_recv()
        s1[p][1, :, pl.ds(0, cut)] = (value[:, :cut] + q1[p][0, :, pl.ds(0, cut)].astype(F32)).astype(BF16)
        s1[p][1, :, pl.ds(cut, sizes[p] - cut)] = value[:, cut:].astype(BF16)
        back1[p][0] = go(s1[p].at[1], q1[p].at[1], nb(d, 1))

    def out_rows(part):
        return inc_ref.at[pl.ds(part * sub, sub), :]

    x_end(va1, va2, mig_a, out_rows(0), out_rows(1))
    y_end(zb1, zb2, mig_b, out_rows(2), out_rows(3))

    for p in (1, 2, 0):
        back1[p][0].wait_recv()
        back1[p][1].wait_recv()
        fin[:, pl.ds(starts[p], sizes[p])] = (
            settle_block(p, 3) + q1[p][1].astype(F32) + q1[p][2].astype(F32)
        )
    last = go(fin.at[pl.ds(pl.multiple_of(8 * oc, 8), 8), :], finr, sibling)
    routed_ref[:, mine] = fin[pl.ds(pl.multiple_of(8 * c, 8), 8), :].astype(BF16)
    last.wait_recv()
    routed_ref[:, other] = finr[...].astype(BF16)
    done_sending()


def finish(a_ref, b_ref, c_ref, x_ref, y_ref, z_ref):
    x_ref[...] = a_ref[...]
    y_ref[...] = b_ref[...]
    z_ref[...] = c_ref[...]


def body(hidden_in, routes, gates, gate_proj, up_proj, down_proj, query, kv_cache, lengths, moving, pair_mask):
    tokens, width = hidden_in.shape
    half = width // 2
    sizes = part_sizes(half)
    ff = gate_proj.shape[2]
    kv_cache, query = jnp.swapaxes(kv_cache, 1, 2), jnp.swapaxes(query, 1, 2)
    requests, kvw, slots = kv_cache.shape
    heads = query.shape[2]
    sub = kvw // 4

    def per_part(*lead, dtype=BF16, extra=False):
        return [
            pltpu.VMEM((*lead, s + (GATE_TILE if extra and p == GATE_PART else 0)), dtype)
            for p, s in enumerate(sizes)
        ]

    mig = (
        [pltpu.VMEM((2, sub, slots), BF16)] * 8
    )
    scratch = [
        *per_part(4, 4, 4, 16, extra=True),
        pltpu.VMEM((half, 4 * ff), BF16),
        pltpu.VMEM((2, ff, half), BF16),
        pltpu.VMEM((4, 4, 4, 16, 4 * ff), F32),
        pltpu.VMEM((4, 4, 4, 16, 2 * ff), F32),
        pltpu.VMEM((2, 4, 4, 4, 16, ff), BF16),
        pltpu.VMEM((2, 4, 4, 4, 16, GATE_TILE), F32),
        pltpu.VMEM((4, 64, max(sizes)), F32),
        *per_part(4, 4, 16),
        *per_part(4, 4, 16),
        *per_part(4, 4, 16),
        *per_part(4, 64, dtype=F32),
        *per_part(3, 4, 16),
        *per_part(3, 4, 16),
        *per_part(3, 16),
        *per_part(3, 16),
        pltpu.VMEM((8, half + GATE_TILE), BF16),
        pltpu.VMEM((8, half + GATE_TILE), BF16),
        pltpu.VMEM((16, half), F32),
        pltpu.VMEM((8, half), F32),
        pltpu.VMEM((requests, kvw, slots), BF16),
        pltpu.VMEM((requests, kvw, heads), BF16),
        *mig,
        *mig,
        pltpu.SemaphoreType.DMA((272,)),
        pltpu.SemaphoreType.DMA((272,)),
        pltpu.SemaphoreType.DMA((8,)),
    ]
    vmem = pl.BlockSpec(memory_space=pltpu.VMEM)
    smem = pl.BlockSpec(memory_space=pltpu.SMEM)
    anywhere = pl.BlockSpec(memory_space=pl.ANY)
    routed, attention, incoming = pl.pallas_call(
        kernel,
        out_shape=(
            jax.ShapeDtypeStruct((tokens, width), BF16),
            jax.ShapeDtypeStruct((requests, heads, LAT), BF16),
            jax.ShapeDtypeStruct((kvw, slots), BF16),
        ),
        in_specs=[vmem, vmem, vmem, anywhere, anywhere, anywhere, anywhere, anywhere, smem, smem, smem],
        out_specs=(vmem, vmem, vmem),
        scratch_shapes=scratch,
        compiler_params=pltpu.CompilerParams(
            collective_id=0, has_side_effects=True, vmem_limit_bytes=64 * 1024 * 1024
        ),
        cost_estimate=pl.CostEstimate(flops=13_000_000_000, bytes_accessed=20_000_000, transcendentals=800_000),
    )(
        hidden_in, routes, gates, gate_proj[0], up_proj[0], down_proj[0], query, kv_cache, lengths, moving, pair_mask
    )
    results = (routed, attention, incoming)
    routed, attention, incoming = pl.pallas_call(
        finish,
        out_shape=tuple(jax.ShapeDtypeStruct(v.shape, v.dtype) for v in results),
        in_specs=[vmem] * 3,
        out_specs=(vmem,) * 3,
    )(*results)
    return routed, attention, incoming.T[None]


def solution(mesh):
    return jax.shard_map(
        body,
        mesh=mesh,
        in_specs=(
            P(("rank", "expert"), None),
            P(("rank", "expert"), None),
            P(("rank", "expert"), None),
            P("expert", None, "rank"),
            P("expert", None, "rank"),
            P("expert", "rank", None),
            P(("rank", "expert"), None, None),
            P(("rank", "expert"), None, None),
            P(("rank", "expert")),
            P(("rank", "expert")),
            P(),
        ),
        out_specs=(
            P(("rank", "expert"), None),
            P(("rank", "expert"), None, None),
            P(("rank", "expert"), None, None),
        ),
        check_vma=False,
    )
```

time: 143 us -> 125 us (0.87)
  local copies, waits for them, and re-layouts: 15.6 us -> 0 us
  Pallas kernels: 125 us -> 123 us
    unnamed x5 -> x0, local copies, waits for them, and re-layouts: 15.6 us -> none
    pallas_call x1, Pallas kernels: 125 us -> 120 us  [body(): pl.pallas_call(kernel, out_shape=(jax.ShapeDtypeStruct((tokens, width), B...]
    pallas_call x0 -> x1, Pallas kernels: none -> 2.73 us  [body(): pl.pallas_call(finish, out_shape=tuple((jax.ShapeDtypeStruct(v.shape, v.d...]
where the time goes in v2:
time: 125 us; the launch traced here: 124 us
  Pallas kernels  123 us (98%)
  between operations  1.93 us (2%)
    pallas_call x1, Pallas kernels, body(): pl.pallas_call(kernel, out_shape=(jax.ShapeDtypeStruct((tokens, width), B...  120 us
    pallas_call x1, Pallas kernels, body(): pl.pallas_call(finish, out_shape=tuple((jax.ShapeDtypeStruct(v.shape, v.d...  2.73 us

profile of v2, /device:TPU:1, one launch (start us, length us, event | category | flops | bytes accessed | tf_op | source)
XLA Modules:
  0.0 124.5 jit_solution(17812365186493214660)
XLA Ops:
  1.9 119.8 %shard_map.130 = (bf16[8,7168]{1,0:T(8,128)(2,1)}, bf16[4,128,512]{2,1,0:T(8,128)(2,1)}, bf16[576,1024]{1,0:T(8,128)(2,1)}) custom-call(bf16[8,7168]{1,0:T(8,128)(2,1)} %hid_ref.1, s32[8,8]{1,0:T(8,128)} %routes_ref.1, bf16[8,8]{1,0:T(8,128)(2,1)} %gates_ref.1, bf16[7168,256]{1,0:T(8,128)(2,1)} %bitcast.9, bf16[7168,256]{1,0:T(8,128)(2,1)} %bitcast.10, ...), custom_call_target="tpu_custom_call" | custom-call | flops 12999999488 | bytes 20000000 | tf_op jit(solution)/shard_map/pallas_call | solution.py:691
  121.8 2.7 %shard_map.131 = (bf16[8,7168]{1,0:T(8,128)(2,1)}, bf16[4,128,512]{2,1,0:T(8,128)(2,1)}, bf16[576,1024]{1,0:T(8,128)(2,1)}) custom-call(bf16[8,7168]{1,0:T(8,128)(2,1)} %get-tuple-element.9.a_ref, bf16[4,128,512]{2,1,0:T(8,128)(2,1)} %get-tuple-element.10.b_ref, bf16[576,1024]{1,0:T(8,128)(2,1)} %get-tuple-element.11.c_ref), custom_call_target="tpu_custom_call" | custom-call | tf_op jit(solution)/shard_map/pallas_call | solution.py:709

commit v3 on v2

--- a/solution.py
+++ b/solution.py
@@ -20,14 +20,14 @@
 
 def part_sizes(half):
     if half == 3584:
-        return (1792, 896, 896)
+        return (1536, 1024, 1024)
     return (half // 3,) * 3
 
 
 def kernel(
     hid_ref, routes_ref, gates_ref, wg_ref, wu_ref, wd_ref, q_ref, kv_ref, len_ref, mov_ref, mask_ref,
     routed_ref, att_ref, inc_ref,
-    x0, x1, x2, w, dn, acc, rb, h, gbuf, tmp,
+    x0, x1, x2, w, dn, acc, rb, h, gbuf, tmp0, tmp1, tmp2,
     f3_0, f3_1, f3_2, r3p_0, r3p_1, r3p_2, r3m_0, r3m_1, r3m_2, t2_0, t2_1, t2_2,
     s2_0, s2_1, s2_2, q2_0, q2_1, q2_2, s1_0, s1_1, s1_2, q1_0, q1_1, q1_2,
     stage_s, stage_r, fin, finr, kvv, qv,
@@ -38,6 +38,7 @@
     sizes = part_sizes(half)
     starts = (0, sizes[0], sizes[0] + sizes[1])
     xs, f3, r3p, r3m = (x0, x1, x2), (f3_0, f3_1, f3_2), (r3p_0, r3p_1, r3p_2), (r3m_0, r3m_1, r3m_2)
+    tmp = (tmp0, tmp1, tmp2)
     t2, s2, q2 = (t2_0, t2_1, t2_2), (s2_0, s2_1, s2_2), (q2_0, q2_1, q2_2)
     s1, q1 = (s1_0, s1_1, s1_2), (q1_0, q1_1, q1_2)
     ff = wg_ref.shape[1]
@@ -382,6 +383,13 @@
         project(p, lines_at(p, 0, range(4)))
     attend(2)
     for p in range(3):
+        for k in range(4):
+            rest_arrived(own3[p][k], k)
+        rest_arrived(g3[p][1], 1)
+        rest_arrived(g3[p][2], 2)
+        project(p, lines_at(p, -1, range(3)) + lines_at(p, 1, range(3)))
+    attend(3)
+    for p in range(3):
         a1, a2, a3 = place(p)
         g3[p][3][0].wait_recv()
         left = xs[p].at[near(a3, -1), near(a2, 2), pl.ds(0, 2)]
@@ -391,19 +399,12 @@
         g3f[p][3] = (one, go(right, right, nb(DIMS[p][2], -1)))
     mig_a = y_second(ya1, ya2, za1, za2, sa, mig_a)
     mig_b = x_second(vb1, vb2, ub, mig_b)
-    for p in range(3):
-        for k in range(4):
-            rest_arrived(own3[p][k], k)
-        rest_arrived(g3[p][1], 1)
-        rest_arrived(g3[p][2], 2)
-        project(p, lines_at(p, -1, range(4)) + lines_at(p, 1, range(4)))
-    attend(3)
     for p in (1, 2, 0):
         for k in range(4):
             own3f[p][k].wait_recv()
         for k in (1, 2):
             g3f[p][k][0].wait_recv()
-        project(p, lines_at(p, 2, range(3)))
+        project(p, lines_at(p, 2, range(3)) + lines_at(p, -1, (3,)) + lines_at(p, 1, (3,)))
     lwd.wait()
     rwd.wait_recv()
     for p in (1, 2, 0):
@@ -417,6 +418,11 @@
         part_sends.append(
             go(acc.at[xx, :, :, :, pl.ds(pl.multiple_of(2 * oc * ff, 128), 2 * ff)], rb.at[xx], sibling)
         )
+
+    y_end(za1, za2, mig_a, va1.at[0], va2.at[0])
+    mig_a = x_first(va1, va2, ua)
+    x_end(vb1, vb2, mig_b, yb1.at[0], yb2.at[0])
+    mig_b = y_first(yb1, yb2)
 
     for n in range(2):
         pick = lax.broadcasted_iota(jnp.int32, (GATE_TILE, GATE_TILE), 0) == e - c + n
@@ -443,7 +449,7 @@
 
         hs = [pull(h, n) for n in range(2)]
         gs = [pull(gbuf, n) for n in range(2)]
-        most = 896 if sizes[p] % 896 == 0 else 256
+        most = sizes[p] if sizes[p] <= 1152 else sizes[p] // 2
         gs = [jnp.concatenate([g] * (most // GATE_TILE), axis=1) for g in gs]
 
         def tile(first, width):
@@ -464,11 +470,6 @@
 
     roffs = (2, -1, 1, 0)
 
-    def down_to_tmp(p, j):
-        view = tmp.at[:, :, pl.ds(0, sizes[p])]
-        down(p, j, view)
-        return view
-
     def put(p, which, k2, value):
         xs[p][which, k2, :, :, : sizes[p]] = value.astype(BF16).reshape(4, 16, sizes[p])
 
@@ -499,48 +500,51 @@
         for k in range(4):
             fw3[p][4 + k] = forward3(a2, near(a1, roffs[k]), 3, side_of(k))
 
-    y_end(za1, za2, mig_a, va1.at[0], va2.at[0])
-    mig_a = x_first(va1, va2, ua)
-    x_end(vb1, vb2, mig_b, yb1.at[0], yb2.at[0])
-    mig_b = y_first(yb1, yb2)
-
     to_side = {1: [[None] * 8 for _ in range(3)], -1: [[None] * 8 for _ in range(3)]}
     back3 = {1: r3p, -1: r3m}
-    for p in (1, 2, 0):
-        a1, a2, a3 = place(p)
-        for side, which in ((1, 1), (-1, 2)):
-            sent = to_side[side][p]
-            view = down_to_tmp(p, near(a3, side))
-            fw3[p][0][0 if side == 1 else 1].wait_recv()
-            value = view[near(a2, 2)]
-            first = 0 if side == 1 else 2
-            added = f3[p][0, pl.ds(first, 2)].reshape(32, sizes[p]).astype(F32)
+    sides = ((1, 1, 2), (-1, 2, 1))
+
+    def line_to(p, side, which, k, added):
+        value = tmp[p][which - 1, near(place(p)[1], roffs[k])]
+        if added:
+            fw3[p][k].wait_recv()
+            value = value + f3[p][k].reshape(64, sizes[p]).astype(F32)
+        put(p, which, k, value)
+        to_side[side][p][k] = send3(p, which, k, pl.ds(0, 4), back3[side], side)
+
+    for p in (1, 2, 0):
+        for side, which, joined in sides:
+            down(p, near(place(p)[2], side), tmp[p].at[which - 1])
+            line_to(p, side, which, 3 - joined, False)
+    for p in (1, 2, 0):
+        for side, which, joined in sides:
+            fw3[p][0][which - 1].wait_recv()
+            value = tmp[p][which - 1, near(place(p)[1], 2)]
+            added = f3[p][0, pl.ds(2 * which - 2, 2)].reshape(32, sizes[p]).astype(F32)
             if side == 1:
                 value = jnp.concatenate([value[:32] + added, value[32:]], axis=0)
             else:
                 value = jnp.concatenate([value[:32], value[32:] + added], axis=0)
             put(p, which, 0, value)
-            sent[0] = send3(p, which, 0, pl.ds(0, 4), back3[side], side)
-            for k in (1, 2):
-                value = view[near(a2, roffs[k])]
-                if side_of(k) == side:
-                    fw3[p][k].wait_recv()
-                    value = value + f3[p][k].reshape(64, sizes[p]).astype(F32)
-                put(p, which, k, value)
-                sent[k] = send3(p, which, k, pl.ds(0, 4), back3[side], side)
-            for k in range(4):
-                i1 = near(a1, roffs[k])
-                value = view[a2, pl.ds(pl.multiple_of(i1 * 16, 16), 16), :]
+            to_side[side][p][0] = send3(p, which, 0, pl.ds(0, 4), back3[side], side)
+    mig_a = x_second(va1, va2, ua, mig_a)
+    mig_b = y_second(yb1, yb2, zb1, zb2, sb, mig_b)
+    for p in (1, 2, 0):
+        for side, which, joined in sides:
+            line_to(p, side, which, joined, True)
+    for p in (1, 2, 0):
+        a1, a2, a3 = place(p)
+        for k in range(4):
+            i1 = near(a1, roffs[k])
+            for side, which, joined in sides:
+                value = tmp[p][which - 1, a2, pl.ds(pl.multiple_of(i1 * 16, 16), 16), :]
                 if side_of(k) == side:
                     fw3[p][4 + k].wait_recv()
                     value = value + f3[p][3, i1].astype(F32)
                 put_block(p, which, 3, i1, value)
-                sent[4 + k] = send3(p, which, 3, i1, back3[side], side)
+                to_side[side][p][4 + k] = send3(p, which, 3, i1, back3[side], side)
     for p in (1, 2, 0):
         down(p, place(p)[2], t2[p])
-
-    mig_a = x_second(va1, va2, ua, mig_a)
-    mig_b = y_second(yb1, yb2, zb1, zb2, sb, mig_b)
 
     def settle(p, k):
         i2 = near(place(p)[1], roffs[k])
@@ -664,7 +668,7 @@
         pltpu.VMEM((4, 4, 4, 16, 2 * ff), F32),
         pltpu.VMEM((2, 4, 4, 4, 16, ff), BF16),
         pltpu.VMEM((2, 4, 4, 4, 16, GATE_TILE), F32),
-        pltpu.VMEM((4, 64, max(sizes)), F32),
+        *per_part(2, 4, 64, dtype=F32),
         *per_part(4, 4, 16),
         *per_part(4, 4, 16),
         *per_part(4, 4, 16),

time: 125 us -> 114 us (0.912)
  Pallas kernels: 123 us -> 112 us
    pallas_call x1, Pallas kernels: 120 us -> 109 us  [body(): pl.pallas_call(kernel, out_shape=(jax.ShapeDtypeStruct((tokens, width), B...]
where the time goes in v3:
time: 114 us
  Pallas kernels  112 us (98%)
  between operations  1.93 us (2%)
    pallas_call x1, Pallas kernels, body(): pl.pallas_call(kernel, out_shape=(jax.ShapeDtypeStruct((tokens, width), B...  109 us
    pallas_call x1, Pallas kernels, body(): pl.pallas_call(finish, out_shape=tuple((jax.ShapeDtypeStruct(v.shape, v.d...  2.73 us

profile of v3, /device:TPU:1, one launch (start us, length us, event | category | flops | bytes accessed | tf_op | source)
XLA Modules:
  0.0 113.8 jit_solution(2299117537879372841)
XLA Ops:
  1.9 109.2 %shard_map.130 = (bf16[8,7168]{1,0:T(8,128)(2,1)}, bf16[4,128,512]{2,1,0:T(8,128)(2,1)}, bf16[576,1024]{1,0:T(8,128)(2,1)}) custom-call(bf16[8,7168]{1,0:T(8,128)(2,1)} %hid_ref.1, s32[8,8]{1,0:T(8,128)} %routes_ref.1, bf16[8,8]{1,0:T(8,128)(2,1)} %gates_ref.1, bf16[7168,256]{1,0:T(8,128)(2,1)} %bitcast.9, bf16[7168,256]{1,0:T(8,128)(2,1)} %bitcast.10, ...), custom_call_target="tpu_custom_call" | custom-call | flops 12999999488 | bytes 20000000 | tf_op jit(solution)/shard_map/pallas_call | solution.py:695
  111.1 2.7 %shard_map.131 = (bf16[8,7168]{1,0:T(8,128)(2,1)}, bf16[4,128,512]{2,1,0:T(8,128)(2,1)}, bf16[576,1024]{1,0:T(8,128)(2,1)}) custom-call(bf16[8,7168]{1,0:T(8,128)(2,1)} %get-tuple-element.9.a_ref, bf16[4,128,512]{2,1,0:T(8,128)(2,1)} %get-tuple-element.10.b_ref, bf16[576,1024]{1,0:T(8,128)(2,1)} %get-tuple-element.11.c_ref), custom_call_target="tpu_custom_call" | custom-call | tf_op jit(solution)/shard_map/pallas_call | solution.py:713

commit v4 on v3

--- a/solution.py
+++ b/solution.py
@@ -108,9 +108,9 @@
     stage_s[:, pl.ds(half, GATE_TILE)] = gate_rows.astype(BF16)
 
     barrier = pltpu.get_barrier_semaphore()
-    for device in (nb(0, 1), nb(0, -1), nb(1, 1), nb(1, -1), nb(2, 1), nb(2, -1), sibling):
+    for device in [nb(dim, delta) for dim in range(3) for delta in (1, -1, 2)] + [sibling]:
         pl.semaphore_signal(barrier, inc=1, device_id=device, device_id_type=MESH)
-    pl.semaphore_wait(barrier, 7)
+    pl.semaphore_wait(barrier, 10)
 
     tok = go(stage_s, stage_r, sibling)
     tok.wait_recv()
@@ -465,9 +465,6 @@
         for first in range(0, sizes[p], most):
             tile(first, most)
 
-    def cut_of(p):
-        return sizes[p] // 256 * 128
-
     roffs = (2, -1, 1, 0)
 
     def put(p, which, k2, value):
@@ -589,32 +586,11 @@
         back2[p][1][k].wait_recv()
         return value + q2[p][1, i1].astype(F32) + q2[p][2, i1].astype(F32)
 
-    fw1, back1 = [None] * 3, [[None, None] for _ in range(3)]
-    for p in (1, 2, 0):
-        d = DIMS[p][0]
-        s1[p][0] = settle_block(p, 0).astype(BF16)
-        cut = cut_of(p)
-        left, right = pl.ds(0, cut), pl.ds(cut, sizes[p] - cut)
-        fw1[p] = (
-            go(s1[p].at[0, :, left], q1[p].at[0, :, left], nb(d, 1)),
-            go(s1[p].at[0, :, right], q1[p].at[0, :, right], nb(d, -1)),
-        )
-    for p in (1, 2, 0):
-        d = DIMS[p][0]
-        cut = cut_of(p)
-        value = settle_block(p, 1)
-        fw1[p][1].wait_recv()
-        s1[p][2, :, pl.ds(0, cut)] = value[:, :cut].astype(BF16)
-        s1[p][2, :, pl.ds(cut, sizes[p] - cut)] = (value[:, cut:] + q1[p][0, :, pl.ds(cut, sizes[p] - cut)].astype(F32)).astype(BF16)
-        back1[p][1] = go(s1[p].at[2], q1[p].at[2], nb(d, -1))
-    for p in (1, 2, 0):
-        d = DIMS[p][0]
-        cut = cut_of(p)
-        value = settle_block(p, 2)
-        fw1[p][0].wait_recv()
-        s1[p][1, :, pl.ds(0, cut)] = (value[:, :cut] + q1[p][0, :, pl.ds(0, cut)].astype(F32)).astype(BF16)
-        s1[p][1, :, pl.ds(cut, sizes[p] - cut)] = value[:, cut:].astype(BF16)
-        back1[p][0] = go(s1[p].at[1], q1[p].at[1], nb(d, 1))
+    sent1 = [[None] * 3 for _ in range(3)]
+    for k, slot, delta in ((0, 0, 2), (1, 2, -1), (2, 1, 1)):
+        for p in (1, 2, 0):
+            s1[p][slot] = settle_block(p, k).astype(BF16)
+            sent1[p][slot] = go(s1[p].at[slot], q1[p].at[slot], nb(DIMS[p][0], delta))
 
     def out_rows(part):
         return inc_ref.at[pl.ds(part * sub, sub), :]
@@ -623,11 +599,11 @@
     y_end(zb1, zb2, mig_b, out_rows(2), out_rows(3))
 
     for p in (1, 2, 0):
-        back1[p][0].wait_recv()
-        back1[p][1].wait_recv()
-        fin[:, pl.ds(starts[p], sizes[p])] = (
-            settle_block(p, 3) + q1[p][1].astype(F32) + q1[p][2].astype(F32)
-        )
+        total = settle_block(p, 3)
+        for slot in range(3):
+            sent1[p][slot].wait_recv()
+            total = total + q1[p][slot].astype(F32)
+        fin[:, pl.ds(starts[p], sizes[p])] = total
     last = go(fin.at[pl.ds(pl.multiple_of(8 * oc, 8), 8), :], finr, sibling)
     routed_ref[:, mine] = fin[pl.ds(pl.multiple_of(8 * c, 8), 8), :].astype(BF16)
     last.wait_recv()

time: 114 us -> 112 us (0.982)
  Pallas kernels: 112 us -> 110 us
    pallas_call x1, Pallas kernels: 109 us -> 107 us  [body(): pl.pallas_call(kernel, out_shape=(jax.ShapeDtypeStruct((tokens, width), B...]
where the time goes in v4:
time: 112 us
  Pallas kernels  110 us (98%)
  between operations  1.93 us (2%)
    pallas_call x1, Pallas kernels, body(): pl.pallas_call(kernel, out_shape=(jax.ShapeDtypeStruct((tokens, width), B...  107 us
    pallas_call x1, Pallas kernels, body(): pl.pallas_call(finish, out_shape=tuple((jax.ShapeDtypeStruct(v.shape, v.d...  2.73 us

profile of v4, /device:TPU:1, one launch (start us, length us, event | category | flops | bytes accessed | tf_op | source)
XLA Modules:
  0.0 112.1 jit_solution(17650329495653969066)
XLA Ops:
  1.9 107.5 %shard_map.130 = (bf16[8,7168]{1,0:T(8,128)(2,1)}, bf16[4,128,512]{2,1,0:T(8,128)(2,1)}, bf16[576,1024]{1,0:T(8,128)(2,1)}) custom-call(bf16[8,7168]{1,0:T(8,128)(2,1)} %hid_ref.1, s32[8,8]{1,0:T(8,128)} %routes_ref.1, bf16[8,8]{1,0:T(8,128)(2,1)} %gates_ref.1, bf16[7168,256]{1,0:T(8,128)(2,1)} %bitcast.9, bf16[7168,256]{1,0:T(8,128)(2,1)} %bitcast.10, ...), custom_call_target="tpu_custom_call" | custom-call | flops 12999999488 | bytes 20000000 | tf_op jit(solution)/shard_map/pallas_call | solution.py:671
  109.4 2.7 %shard_map.131 = (bf16[8,7168]{1,0:T(8,128)(2,1)}, bf16[4,128,512]{2,1,0:T(8,128)(2,1)}, bf16[576,1024]{1,0:T(8,128)(2,1)}) custom-call(bf16[8,7168]{1,0:T(8,128)(2,1)} %get-tuple-element.9.a_ref, bf16[4,128,512]{2,1,0:T(8,128)(2,1)} %get-tuple-element.10.b_ref, bf16[576,1024]{1,0:T(8,128)(2,1)} %get-tuple-element.11.c_ref), custom_call_target="tpu_custom_call" | custom-call | tf_op jit(solution)/shard_map/pallas_call | solution.py:689

commit v5 on v4

--- a/solution.py
+++ b/solution.py
@@ -338,13 +338,6 @@
             g2f[p][k].wait_recv()
         third_line(p, 3)
 
-    pick_rows(ya1, 0, 0)
-    pick_rows(ya2, 0, 1)
-    mig_a = y_first(ya1, ya2)
-    pick_rows(vb1, 0, 2)
-    pick_rows(vb2, 0, 3)
-    mig_b = x_first(vb1, vb2, ub)
-
     def rows_of(p, j):
         full = slice(None)
         if p == 0:
@@ -379,6 +372,13 @@
     for p in range(3):
         line_on(p, 1)
         line_on(p, 2)
+    pick_rows(ya1, 0, 0)
+    pick_rows(ya2, 0, 1)
+    mig_a = y_first(ya1, ya2)
+    pick_rows(vb1, 0, 2)
+    pick_rows(vb2, 0, 3)
+    mig_b = x_first(vb1, vb2, ub)
+
     for p in range(3):
         project(p, lines_at(p, 0, range(4)))
     attend(2)

time: 112 us -> 113 us (level)
  no operation moved by 1% of the time
where the time goes in v5:
time: 113 us
  Pallas kernels  111 us (98%)
  between operations  1.93 us (2%)
    pallas_call x1, Pallas kernels, body(): pl.pallas_call(kernel, out_shape=(jax.ShapeDtypeStruct((tokens, width), B...  108 us
    pallas_call x1, Pallas kernels, body(): pl.pallas_call(finish, out_shape=tuple((jax.ShapeDtypeStruct(v.shape, v.d...  2.73 us

profile of v5, /device:TPU:1, one launch (start us, length us, event | category | flops | bytes accessed | tf_op | source)
XLA Modules:
  0.0 112.8 jit_solution(11491930729871370715)
XLA Ops:
  1.9 108.1 %shard_map.130 = (bf16[8,7168]{1,0:T(8,128)(2,1)}, bf16[4,128,512]{2,1,0:T(8,128)(2,1)}, bf16[576,1024]{1,0:T(8,128)(2,1)}) custom-call(bf16[8,7168]{1,0:T(8,128)(2,1)} %hid_ref.1, s32[8,8]{1,0:T(8,128)} %routes_ref.1, bf16[8,8]{1,0:T(8,128)(2,1)} %gates_ref.1, bf16[7168,256]{1,0:T(8,128)(2,1)} %bitcast.9, bf16[7168,256]{1,0:T(8,128)(2,1)} %bitcast.10, ...), custom_call_target="tpu_custom_call" | custom-call | flops 12999999488 | bytes 20000000 | tf_op jit(solution)/shard_map/pallas_call | solution.py:671
  110.1 2.7 %shard_map.131 = (bf16[8,7168]{1,0:T(8,128)(2,1)}, bf16[4,128,512]{2,1,0:T(8,128)(2,1)}, bf16[576,1024]{1,0:T(8,128)(2,1)}) custom-call(bf16[8,7168]{1,0:T(8,128)(2,1)} %get-tuple-element.9.a_ref, bf16[4,128,512]{2,1,0:T(8,128)(2,1)} %get-tuple-element.10.b_ref, bf16[576,1024]{1,0:T(8,128)(2,1)} %get-tuple-element.11.c_ref), custom_call_target="tpu_custom_call" | custom-call | tf_op jit(solution)/shard_map/pallas_call | solution.py:689
